TPU v7x, 128 devices: a whole 4x4x4 slice. The times are simulated.
128 devices in a mesh: dp: 32 (over z, y, core), expert: 2 (over x_hi), tensor: 2 (over x_lo).
Axes of the slice: x: 4 (x_hi: 2, x_lo: 2; x = x_hi * 2 + x_lo), y: 4, z: 4, core: 2. Of those that a mesh axis runs over, the one named last changes fastest.
Arguments:
- tokens: bfloat16 [2048, 4096], P('dp', 'tensor'), may hold values from -6 to 6
- targets: bfloat16 [2048, 4096], P('dp', 'tensor'), may hold values from -6 to 6
- norm_gain: float32 [4096], P('tensor'), may hold values from 0.1 to 1.9
- expert_ids: int32 [2048, 2], P('dp'), may hold values from 0 to 7, all different within a row; in each aligned block of 64 rows (0 to 63, 64 to 127, ...) at most 18 rows name the same one
- gate_prob: float32 [2048, 2], P('dp'), may hold values from 0.2 to 1
- w_gate: bfloat16 [4096, 65536], P('tensor', ('dp', 'expert')), may hold values from -0.09375 to 0.09375
- gate_probe: bfloat16 [4096, 65536], P('tensor', ('dp', 'expert')), as said below
- w_up: bfloat16 [4096, 65536], P('tensor', ('dp', 'expert')), may hold values from -0.09375 to 0.09375
- w_down: bfloat16 [65536, 4096], P(('dp', 'expert'), 'tensor'), may hold values from -0.0625 to 0.0625
Outputs:
- normed: bfloat16 [2048, 4096], P('dp', 'tensor')
- curvature: float32 [2048, 2], P('dp')
- estimate: float32 [8], replicated
Inputs may be any that keep to these rules, and one draw needn't show every extreme that they name: `expert_ids`: the two ids of a token differ; within each block of 64 consecutive tokens no expert is named more than 18 times; every expert is named by some token. `gate_probe`: every entry is plus or minus 1 / sqrt(4096).
All inputs are finite; a program needn't handle non-finite values.
Results may differ from a plain program's by a relative error of at most 0.03.
Values may be sent and summed in bfloat16 or wider, within the bound.
A program may use at most 128 MiB of HBM per device.

v0:
```python
import jax
import jax.numpy as jnp
from jax import lax
from jax.sharding import PartitionSpec as P

D = 4096
EXPERTS = 8
CAP = 18


epsilon = 1e-05
loss_weight = 8.0


def sent_to_all(x, axis):
    copies = jnp.broadcast_to(x, (lax.axis_size(axis), *x.shape))
    return lax.all_to_all(copies, axis, split_axis=0, concat_axis=0, tiled=True)


def of_everyone(x, axis):
    everything = sent_to_all(x, axis)
    return jnp.sum(everything.astype(jnp.float32), axis=0)


def of_everyone_2(x, axis):
    everything = sent_to_all(x, axis)
    return jnp.sum(everything, axis=0)


def packed_total(arrays, axis):
    ends = [0]
    for a in arrays:
        ends.append(ends[-1] + a.size)
    running = of_everyone_2(jnp.concatenate([a.ravel() for a in arrays]), axis)
    return tuple((running[b:e].reshape(a.shape) for a, b, e in zip(arrays, ends, ends[1:])))


def derivative_jets(preact):
    gate_in = preact[:, 0]
    gate_dir = preact[:, 1]
    up_in = preact[:, 2]
    sigmoid_in = jax.nn.sigmoid(gate_in)
    first_slope = sigmoid_in * (1.0 + gate_in * (1.0 - sigmoid_in))
    second_slope = sigmoid_in * (1.0 - sigmoid_in) * (2.0 + gate_in * (1.0 - 2.0 * sigmoid_in))
    primal = gate_in * sigmoid_in * up_in
    tangent = first_slope * gate_dir * up_in
    second = second_slope * gate_dir * gate_dir * up_in
    return jnp.stack([primal, tangent, second], axis=1).astype(jnp.bfloat16)


def slot_numbers(flat_ids):
    onehot = (flat_ids[:, None] == jnp.arange(EXPERTS, dtype=jnp.int32)[None, :]).astype(jnp.int32)
    before = jnp.cumsum(onehot, axis=0) - onehot
    return jnp.sum(before * onehot, axis=1)


def slot_curvature(inv_root, moments, weighted_uu, resid_b, resid_a, resid_u):
    inv_cube = inv_root * inv_root * inv_root
    first_rate = 2.0 * moments[..., 0] / D
    second_rate = 2.0 * (moments[..., 1] + moments[..., 2]) / D
    slope_one = -0.5 * inv_cube * first_rate
    slope_two = (
        0.75 * inv_cube * inv_root * inv_root * first_rate * first_rate
        - 0.5 * inv_cube * second_rate
    )
    tangent_sq = (
        inv_root * inv_root * moments[..., 3]
        + 2.0 * inv_root * slope_one * moments[..., 4]
        + slope_one * slope_one * weighted_uu
    )
    bending = inv_root * resid_b + 2.0 * slope_one * resid_a + slope_two * resid_u
    return 2.0 * loss_weight / D * (tangent_sq + bending)


def on_device(tokens, targets, norm_gain, expert_ids, gate_prob, w_gate, gate_probe, w_up, w_down):
    tok_rows, width_part = tokens.shape
    hidden_part = w_gate.shape[1]
    holders = lax.axis_size("dp") // EXPERTS
    flat_ids = expert_ids.reshape(-1)
    places = flat_ids * CAP + slot_numbers(flat_ids)
    outgoing = (
        jnp.zeros((EXPERTS * CAP, width_part), jnp.bfloat16)
        .at[places]
        .set(jnp.repeat(tokens, 2, axis=0))
    )
    outgoing = jnp.repeat(outgoing.reshape(EXPERTS, CAP, width_part), holders, axis=0)
    arrived = lax.all_to_all(outgoing, "dp", split_axis=0, concat_axis=0, tiled=True)
    senders = arrived.shape[0]
    expert_rows = arrived.reshape(senders * CAP, width_part)
    partial_value = jnp.stack(
        [
            jnp.dot(expert_rows, w_gate, preferred_element_type=jnp.float32),
            jnp.dot(expert_rows, gate_probe, preferred_element_type=jnp.float32),
            jnp.dot(expert_rows, w_up, preferred_element_type=jnp.float32),
        ],
        axis=1,
    )
    hidden_jets = derivative_jets(
        of_everyone(partial_value.astype(jnp.bfloat16), "tensor").astype(jnp.float32)
    )
    images = jnp.dot(
        hidden_jets.reshape(-1, hidden_part), w_down, preferred_element_type=jnp.float32
    )
    images = images.reshape(senders, CAP, 3, width_part).astype(jnp.bfloat16)
    returned = lax.all_to_all(images, "dp", split_axis=0, concat_axis=0, tiled=True)
    grouped = jnp.sum(
        returned.astype(jnp.float32).reshape(EXPERTS, holders, CAP, 3, width_part), axis=1
    )
    expert_table = of_everyone(grouped.astype(jnp.bfloat16), "expert").astype(jnp.float32)
    picked = expert_table.reshape(EXPERTS * CAP, 3, width_part)[places].reshape(
        tok_rows, 2, 3, width_part
    )
    weights = gate_prob[:, :, None]
    summed = tokens.astype(jnp.float32) + jnp.sum(weights * picked[:, :, 0], axis=1)
    tangent_out = weights * picked[:, :, 1]
    second_out = weights * picked[:, :, 2]
    target = targets.astype(jnp.float32)
    gain_sq = norm_gain * norm_gain
    spread_sum = summed[:, None, :]
    cross_ua = jnp.sum(spread_sum * tangent_out, axis=-1)
    along_aa = jnp.sum(tangent_out * tangent_out, axis=-1)
    cross_ub = jnp.sum(spread_sum * second_out, axis=-1)
    weighted_aa = jnp.sum(gain_sq * tangent_out * tangent_out, axis=-1)
    weighted_au = jnp.sum(gain_sq * spread_sum * tangent_out, axis=-1)
    gain_target = norm_gain * target
    weighted_ub = jnp.sum(gain_sq * spread_sum * second_out, axis=-1)
    target_b = jnp.sum(gain_target[:, None, :] * second_out, axis=-1)
    target_a = jnp.sum(gain_target[:, None, :] * tangent_out, axis=-1)
    token_stats = jnp.stack(
        [
            jnp.sum(summed * summed, axis=-1),
            jnp.sum(gain_sq * summed * summed, axis=-1),
            jnp.sum(gain_target * summed, axis=-1),
        ],
        axis=-1,
    )
    slot_stats = jnp.stack(
        [cross_ua, along_aa, cross_ub, weighted_aa, weighted_au, weighted_ub, target_b, target_a],
        axis=-1,
    )
    slot_total, token_total = packed_total((slot_stats, token_stats), "tensor")
    inv_root = lax.rsqrt(token_total[:, 0] / D + epsilon)[:, None]
    weighted_uu = token_total[:, 1:2]
    resid_b = inv_root * slot_total[..., 5] - slot_total[..., 6]
    resid_a = inv_root * slot_total[..., 4] - slot_total[..., 7]
    resid_u = inv_root * weighted_uu - token_total[:, 2:3]
    scaled = norm_gain * summed * inv_root
    normed = scaled.astype(jnp.bfloat16)
    curvature = slot_curvature(
        inv_root, slot_total[..., :5], weighted_uu, resid_b, resid_a, resid_u
    )
    member = (expert_ids[:, :, None] == jnp.arange(EXPERTS, dtype=jnp.int32)).astype(jnp.float32)
    totals, counts = packed_total(
        (jnp.sum(member * curvature[:, :, None], axis=(0, 1)), jnp.sum(member, axis=(0, 1))), "dp"
    )
    return (normed, curvature, totals / counts)


def solution(mesh):
    return jax.shard_map(
        on_device,
        mesh=mesh,
        in_specs=(
            P("dp", "tensor"),
            P("dp", "tensor"),
            P("tensor"),
            P("dp", None),
            P("dp", None),
            P("tensor", ("dp", "expert")),
            P("tensor", ("dp", "expert")),
            P("tensor", ("dp", "expert")),
            P(("dp", "expert"), "tensor"),
        ),
        out_specs=(P("dp", "tensor"), P("dp", None), P()),
        check_vma=False,
    )
```

profile of v0, /device:TPU:1, one launch (start us, length us, event | category | flops | bytes accessed | tf_op | source)
XLA Modules:
  0.0 407.6 jit_solution(8891842776413838986)
XLA Ops:
  7.0 49.0 %all_to_all.32 = bf16[32,18,2048]{2,1,0:T(8,128)(2,1)S(1)} all-to-all(bf16[32,18,2048]{2,1,0:T(8,128)(2,1)S(1)} %bitcast.156), channel_id=1, replica_groups=mesh['dp'=32,'expert'=2,'tensor'=2] {'dp'}, dimensions={0} | all-to-all | bytes 4718592 | tf_op jit(solution)/shard_map/all_to_all | solution.py:87
  56.1 2.2 reshape.180
  58.3 5.6 %fusion.10 = bf16[576,1,1024]{2,0,1:T(8,128)(2,1)S(1)} fusion(bf16[576,2048]{1,0:T(8,128)(2,1)} %reshape.180, bf16[2048,1024]{1,0:T(8,128)(2,1)} %param.14), kind=kOutput, calls=%fused_computation.27 | convolution fusion | flops 2416508928 | bytes 7733248 | tf_op jit(solution)/shard_map/dot_general | solution.py:92
  64.0 2.6 fusion.11
  66.6 2.6 fusion.12
  70.7 80.9 %all_to_all.33 = bf16[2,576,3,1024]{3,1,2,0:T(8,128)(2,1)S(1)} all-to-all(bf16[2,576,3,1024]{3,1,2,0:T(8,128)(2,1)S(1)} %broadcast_in_dim.17), channel_id=1, replica_groups=mesh['dp'=32,'expert'=2,'tensor'=2] {'tensor'}, dimensions={0} | all-to-all | bytes 14155776 | tf_op jit(solution)/shard_map/all_to_all | solution.py:17
  151.6 1.9 convert_reduce_fusion
  153.6 1.9 multiply_convert_fusion
  155.9 3.5 convert_element_type.38
  159.3 12.2 %convolution_convert_fusion = bf16[32,18,3,2048]{3,0,2,1:T(8,128)(2,1)S(1)} fusion(bf16[1024,2048]{1,0:T(8,128)(2,1)} %param.17, bf16[32,18,3,1024]{3,1,0,2:T(8,128)(2,1)} %convert_element_type.38), kind=kOutput, calls=%fused_computation.5 | convolution fusion | flops 7251296256 | bytes 14811136 | tf_op jit(solution)/shard_map/dot_general | solution.py:101
  171.5 15.8 %copy.177 = bf16[32,18,3,2048]{3,2,1,0:T(4,128)(2,1)S(1)} copy(bf16[32,18,3,2048]{3,0,2,1:T(8,128)(2,1)S(1)} %convolution_convert_fusion) | data formatting | bytes 14155776 | tf_op jit(solution)/shard_map/convert_element_type | solution.py:104
  187.3 111.7 %all_to_all.34 = bf16[32,18,3,2048]{3,2,1,0:T(4,128)(2,1)S(1)} all-to-all(bf16[32,18,3,2048]{3,2,1,0:T(4,128)(2,1)S(1)} %copy.177), channel_id=1, replica_groups=mesh['dp'=32,'expert'=2,'tensor'=2] {'dp'}, dimensions={0} | all-to-all | bytes 14155776 | tf_op jit(solution)/shard_map/all_to_all | solution.py:105
  299.0 6.3 %bitcast_reduce_fusion = bf16[8,18,3,2048]{3,2,1,0:T(4,128)(2,1)S(1)} fusion(bf16[32,18,3,2048]{3,2,1,0:T(4,128)(2,1)S(1)} %all_to_all.34), kind=kLoop, calls=%fused_computation.3 | loop fusion | flops 2654208 | bytes 8847360 | tf_op jit(solution)/shard_map/reduce_sum | solution.py:106
  306.8 2.3 broadcast_in_dim.18
  309.2 4.4 %all-to-all-start.3 = ((bf16[2,8,18,3,2048]{4,1,3,2,0:T(8,128)(2,1)}), bf16[2,8,18,3,2048]{4,1,3,2,0:T(8,128)(2,1)S(1)}, u32[]{:S(2)}, u32[]{:S(2)}) async-start(bf16[2,8,18,3,2048]{4,1,3,2,0:T(8,128)(2,1)} %broadcast_in_dim.18), calls=%async_computation.3 | async-start | bytes 7077888 | tf_op jit(solution)/shard_map/all_to_all | solution.py:17
  315.5 39.0 %all-to-all-done.3 = bf16[2,8,18,3,2048]{4,1,3,2,0:T(8,128)(2,1)S(1)} async-done(((bf16[2,8,18,3,2048]{4,1,3,2,0:T(8,128)(2,1)}), bf16[2,8,18,3,2048]{4,1,3,2,0:T(8,128)(2,1)S(1)}, u32[]{:S(2)}, u32[]{:S(2)}) %all-to-all-start.3) | async-done | bytes 3538976 | tf_op jit(solution)/shard_map/all_to_all | solution.py:17
  355.3 4.6 %copy.179 = f32[8,18,3,2048]{3,2,1,0:T(4,128)} copy(f32[8,18,3,2048]{3,0,2,1:T(8,128)S(1)} %convert_reduce_fusion.1) | data formatting | bytes 7077888 | tf_op jit(solution)/shard_map/reduce_sum | solution.py:22
  359.9 7.3 %gather_fusion = f32[128,3,2048]{2,1,0:T(4,128)} fusion(f32[144,3,2048]{2,1,0:T(4,128)} %bitcast.154, s32[1024]{0:T(1024)} %pad_clamp_fusion), kind=kCustom, calls=%fused_computation | custom fusion | bytes 6291968 | tf_op jit(solution)/shard_map/gather | solution.py:110
  367.2 8.2 %fusion.42 = (f32[64,2,1,2048]{3,2,1,0:T(1,128)S(1)}, f32[64,2,1,2048]{3,2,1,0:T(1,128)S(1)}, f32[64,2,1,2048]{3,2,1,0:T(1,128)S(1)}) fusion(f32[64,2,3,2048]{3,2,1,0:T(4,128)} %bitcast.155), kind=kLoop, calls=%fused_computation.118 | loop fusion | bytes 6291456 | tf_op jit(solution)/shard_map/slice | solution.py:115
  375.4 2.3 fusion.17
  378.1 5.0 %multiply_reduce_fusion.1 = (f32[64,2]{1,0:T(8,128)S(1)}, f32[64,2]{1,0:T(8,128)S(1)}, f32[64,2]{1,0:T(8,128)S(1)}, f32[64,2]{1,0:T(8,128)S(1)}, f32[64,2]{1,0:T...) fusion(f32[64,2048]{1,0:T(8,128)S(1)} %get-tuple-element.37, ...), kind=kLoop, calls=%fused_computation.39 | loop fusion | flops 4979712 | bytes 3682816 | tf_op jit(solution)/shard_map/reduce_sum | solution.py:127
  384.4 5.0 %all_to_all.35 = f32[2,1,1216]{2,1,0:T(1,128)S(1)} all-to-all(f32[2,1,1216]{2,1,0:T(1,128)S(1)} %broadcast_in_dim.19), channel_id=1, replica_groups=mesh['dp'=32,'expert'=2,'tensor'=2] {'tensor'}, dimensions={0} | all-to-all | bytes 19456 | tf_op jit(solution)/shard_map/all_to_all | solution.py:17
  393.0 7.1 %all-to-all-start.5 = ((f32[32,1,16]{2,1,0:T(1,128)}), f32[32,1,16]{2,1,0:T(1,128)S(1)}, u32[]{:S(2)}, u32[]{:S(2)}) async-start(f32[32,1,16]{2,1,0:T(1,128)} %broadcast_in_dim.20), calls=%async_computation.5 | async-start | bytes 32768 | tf_op jit(solution)/shard_map/all_to_all | solution.py:17
  400.6 6.4 %all-to-all-done.5 = f32[32,1,16]{2,1,0:T(1,128)S(1)} async-done(((f32[32,1,16]{2,1,0:T(1,128)}), f32[32,1,16]{2,1,0:T(1,128)S(1)}, u32[]{:S(2)}, u32[]{:S(2)}) %all-to-all-start.5) | async-done | bytes 2080 | tf_op jit(solution)/shard_map/all_to_all | solution.py:17
  (90 shorter events, 18.7 us)
Async XLA Ops:
  4.4 0.5 copy-start.7
  58.3 5.7 %copy-start = (bf16[576,2048]{1,0:T(8,128)(2,1)S(1)}, bf16[576,2048]{1,0:T(8,128)(2,1)}, u32[]{:S(2)}) copy-start(bf16[576,2048]{1,0:T(8,128)(2,1)} %reshape.180) | copy-start | bytes 7077892
  58.3 5.7 %copy-start.8 = (bf16[2048,1024]{1,0:T(8,128)(2,1)S(1)}, bf16[2048,1024]{1,0:T(8,128)(2,1)}, u32[]{:S(2)}) copy-start(bf16[2048,1024]{1,0:T(8,128)(2,1)} %param.15) | copy-start | bytes 12582916
  64.0 2.7 copy-start.9
  309.2 4.4 %copy-start.6 = (f32[64,2]{0,1:T(2,128)S(1)}, f32[64,2]{0,1:T(2,128)}, u32[]{:S(2)}) copy-start(f32[64,2]{0,1:T(2,128)} %param.13) | copy-start | bytes 1540
  309.2 5.1 %copy-start.4 = (f32[2048]{0:T(1024)S(1)}, f32[2048]{0:T(1024)}, u32[]{:S(2)}) copy-start(f32[2048]{0:T(1024)} %param.11) | copy-start | bytes 24580
  309.2 45.3 %all-to-all-start.3 = ((bf16[2,8,18,3,2048]{4,1,3,2,0:T(8,128)(2,1)}), bf16[2,8,18,3,2048]{4,1,3,2,0:T(8,128)(2,1)S(1)}, u32[]{:S(2)}, u32[]{:S(2)}) async-start(bf16[2,8,18,3,2048]{4,1,3,2,0:T(8,128)(2,1)} %broadcast_in_dim.18), calls=%async_computation.3 | async-start | bytes 7077888 | tf_op jit(solution)/shard_map/all_to_all | solution.py:17
  367.2 8.2 %copy-start.2 = (f32[64,2]{1,0:T(8,128)S(1)}, f32[64,2]{1,0:T(8,128)}, u32[]{:S(2)}) copy-start(f32[64,2]{1,0:T(8,128)} %copy.173) | copy-start | bytes 1540
  367.2 10.6 %copy-start.1 = (bf16[64,2048]{1,0:T(8,128)(2,1)S(1)}, bf16[64,2048]{1,0:T(8,128)(2,1)}, u32[]{:S(2)}) copy-start(bf16[64,2048]{1,0:T(8,128)(2,1)} %param.9) | copy-start | bytes 786436
  375.4 2.4 copy-start.3
  378.1 14.0 %copy-start.5 = (s32[64,2]{0,1:T(2,128)S(1)}, s32[64,2]{0,1:T(2,128)}, u32[]{:S(2)}) copy-start(s32[64,2]{0,1:T(2,128)} %param.12) | copy-start | bytes 1540
  393.0 14.0 %all-to-all-start.5 = ((f32[32,1,16]{2,1,0:T(1,128)}), f32[32,1,16]{2,1,0:T(1,128)S(1)}, u32[]{:S(2)}, u32[]{:S(2)}) async-start(f32[32,1,16]{2,1,0:T(1,128)} %broadcast_in_dim.20), calls=%async_computation.5 | async-start | bytes 32768 | tf_op jit(solution)/shard_map/all_to_all | solution.py:17
where the time goes:
time: 408 us
  blocking collectives  247 us (61%)
  local copies, waits for them, and re-layouts  55.6 us (14%)
  waiting for transfers between devices  45.3 us (11%)
  other arithmetic  24.5 us (6%)
  matrix products  23.1 us (6%)
  starting transfers between devices  11.4 us (3%)
    all_to_all x1, blocking collectives, on_device(): lax.all_to_all(images, 'dp', split_axis=0, concat_axis=0, tiled=True)  112 us
    all_to_all x2, blocking collectives, sent_to_all(): return lax.all_to_all(copies, axis, split_axis=0, concat_axis=0, tiled=True)  85.9 us
    all_to_all x1, blocking collectives, on_device(): lax.all_to_all(outgoing, 'dp', split_axis=0, concat_axis=0, tiled=True)  49 us
    all_to_all x2, waiting for transfers between devices, sent_to_all(): return lax.all_to_all(copies, axis, split_axis=0, concat_axis=0, tiled=True)  45.3 us
    convert_element_type x1, local copies, waits for them, and re-layouts, on_device(): images = images.reshape(senders, CAP, 3, width_part).astype(jnp.bfloat16)  15.8 us
    dot_general x1, matrix products, on_device(): jnp.dot(hidden_jets.reshape(-1, hidden_part), w_down, preferred_element_t...  12.2 us
    all_to_all x2, starting transfers between devices, sent_to_all(): return lax.all_to_all(copies, axis, split_axis=0, concat_axis=0, tiled=True)  11.4 us
    slice x1, local copies, waits for them, and re-layouts, on_device(): tangent_out = weights * picked[:, :, 1]  8.2 us
  transfers between devices with their start and end apart: 2, of which 2 were waited for; matrix products, arithmetic and copies ran while one was open for 1% of the time, Pallas kernels for 0%

commit v1 on v0

--- a/solution.py
+++ b/solution.py
@@ -49,9 +49,9 @@
 
 
 def slot_numbers(flat_ids):
-    onehot = (flat_ids[:, None] == jnp.arange(EXPERTS, dtype=jnp.int32)[None, :]).astype(jnp.int32)
-    before = jnp.cumsum(onehot, axis=0) - onehot
-    return jnp.sum(before * onehot, axis=1)
+    number = jnp.arange(flat_ids.shape[0], dtype=jnp.int32)
+    same = flat_ids[:, None] == flat_ids[None, :]
+    return jnp.sum((same & (number[None, :] < number[:, None])).astype(jnp.int32), axis=1)
 
 
 def slot_curvature(inv_root, moments, weighted_uu, resid_b, resid_a, resid_u):
@@ -78,11 +78,12 @@
     holders = lax.axis_size("dp") // EXPERTS
     flat_ids = expert_ids.reshape(-1)
     places = flat_ids * CAP + slot_numbers(flat_ids)
-    outgoing = (
-        jnp.zeros((EXPERTS * CAP, width_part), jnp.bfloat16)
-        .at[places]
-        .set(jnp.repeat(tokens, 2, axis=0))
-    )
+    select = (places[:, None] == jnp.arange(EXPERTS * CAP, dtype=jnp.int32)).astype(jnp.bfloat16)
+    outgoing = jnp.dot(
+        jnp.sum(select.reshape(tok_rows, 2, -1), axis=1).astype(jnp.bfloat16).T,
+        tokens,
+        preferred_element_type=jnp.float32,
+    ).astype(jnp.bfloat16)
     outgoing = jnp.repeat(outgoing.reshape(EXPERTS, CAP, width_part), holders, axis=0)
     arrived = lax.all_to_all(outgoing, "dp", split_axis=0, concat_axis=0, tiled=True)
     senders = arrived.shape[0]
@@ -106,10 +107,9 @@
     grouped = jnp.sum(
         returned.astype(jnp.float32).reshape(EXPERTS, holders, CAP, 3, width_part), axis=1
     )
-    expert_table = of_everyone(grouped.astype(jnp.bfloat16), "expert").astype(jnp.float32)
-    picked = expert_table.reshape(EXPERTS * CAP, 3, width_part)[places].reshape(
-        tok_rows, 2, 3, width_part
-    )
+    grouped = grouped.astype(jnp.bfloat16).reshape(EXPERTS * CAP, 3 * width_part)
+    chosen = jnp.dot(select, grouped, preferred_element_type=jnp.float32).astype(jnp.bfloat16)
+    picked = of_everyone(chosen, "expert").reshape(tok_rows, 2, 3, width_part)
     weights = gate_prob[:, :, None]
     summed = tokens.astype(jnp.float32) + jnp.sum(weights * picked[:, :, 0], axis=1)
     tangent_out = weights * picked[:, :, 1]

time: 408 us -> 403 us (0.988)
  blocking collectives: 247 us -> 135 us
  waiting for transfers between devices: 45.3 us -> 149 us
  local copies, waits for them, and re-layouts: 55.6 us -> 34.6 us
  starting transfers between devices: 11.4 us -> 28.2 us
  other arithmetic: 24.5 us -> 29.1 us
    all_to_all x0 -> x1, waiting for transfers between devices: none -> 113 us  [on_device(): lax.all_to_all(images, 'dp', split_axis=0, concat_axis=0, tiled=True)]
    all_to_all x1 -> x0, blocking collectives: 112 us -> none  [on_device(): lax.all_to_all(images, 'dp', split_axis=0, concat_axis=0, tiled=True)]
    all_to_all x2, starting transfers between devices: 11.4 us -> 22.4 us  [sent_to_all(): return lax.all_to_all(copies, axis, split_axis=0, concat_axis=0, tiled=True)]
    all_to_all x2, waiting for transfers between devices: 45.3 us -> 36.6 us  [sent_to_all(): return lax.all_to_all(copies, axis, split_axis=0, concat_axis=0, tiled=True)]
    convert_element_type x1, local copies, waits for them, and re-layouts: 15.8 us -> 7.27 us  [on_device(): images = images.reshape(senders, CAP, 3, width_part).astype(jnp.bfloat16)]
    gather x1 -> x0, local copies, waits for them, and re-layouts: 7.26 us -> none  [on_device(): expert_table.reshape(EXPERTS * CAP, 3, width_part)[places]]
    all_to_all x0 -> x1, starting transfers between devices: none -> 5.79 us  [on_device(): lax.all_to_all(images, 'dp', split_axis=0, concat_axis=0, tiled=True)]
    reduce_sum x1 -> x2, local copies, waits for them, and re-layouts: 4.55 us -> 0.21 us  [slot_numbers(): jnp.sum((same & (number[None, :] < number[:, None])).astype(jnp.int32), a...]
  transfers between devices with their start and end apart: 2 -> 3, of which waited for: 2 -> 3; matrix products, arithmetic and copies ran while one was open for 1% -> 0% of each run, Pallas kernels for 0% -> 0%
where the time goes in v1:
time: 403 us; the launch traced here: 402 us
  waiting for transfers between devices  149 us (37%)
  blocking collectives  135 us (33%)
  local copies, waits for them, and re-layouts  34.6 us (9%)
  other arithmetic  29.1 us (7%)
  starting transfers between devices  28.2 us (7%)
  matrix products  25 us (6%)
    all_to_all x1, waiting for transfers between devices, on_device(): lax.all_to_all(images, 'dp', split_axis=0, concat_axis=0, tiled=True)  113 us
    all_to_all x2, blocking collectives, sent_to_all(): return lax.all_to_all(copies, axis, split_axis=0, concat_axis=0, tiled=True)  85.9 us
    all_to_all x1, blocking collectives, on_device(): lax.all_to_all(outgoing, 'dp', split_axis=0, concat_axis=0, tiled=True)  49.1 us
    all_to_all x2, waiting for transfers between devices, sent_to_all(): return lax.all_to_all(copies, axis, split_axis=0, concat_axis=0, tiled=True)  36.6 us
    all_to_all x2, starting transfers between devices, sent_to_all(): return lax.all_to_all(copies, axis, split_axis=0, concat_axis=0, tiled=True)  22.4 us
    dot_general x1, matrix products, on_device(): jnp.dot(hidden_jets.reshape(-1, hidden_part), w_down, preferred_element_t...  12.2 us
    reduce_sum x1, other arithmetic, on_device(): jnp.sum(returned.astype(jnp.float32).reshape(EXPERTS, holders, CAP, 3, wi...  10.4 us
    slice x1, local copies, waits for them, and re-layouts, on_device(): tangent_out = weights * picked[:, :, 1]  8.25 us
  transfers between devices with their start and end apart: 3, of which 3 were waited for; matrix products, arithmetic and copies ran while one was open for 0% of the time, Pallas kernels for 0%

profile of v1, /device:TPU:1, one launch (start us, length us, event | category | flops | bytes accessed | tf_op | source)
XLA Modules:
  0.0 402.0 jit_solution(10722697518026133693)
XLA Ops:
  4.6 49.1 %all_to_all.32 = bf16[32,18,2048]{2,1,0:T(8,128)(2,1)S(1)} all-to-all(bf16[32,18,2048]{2,1,0:T(8,128)(2,1)S(1)} %bitcast.150), channel_id=1, replica_groups=mesh['dp'=32,'expert'=2,'tensor'=2] {'dp'}, dimensions={0} | all-to-all | bytes 4718592 | tf_op jit(solution)/shard_map/all_to_all | solution.py:88
  53.6 2.2 reshape.170
  55.9 5.6 %fusion.10 = bf16[576,1,1024]{2,0,1:T(8,128)(2,1)S(1)} fusion(bf16[576,2048]{1,0:T(8,128)(2,1)} %reshape.170, bf16[2048,1024]{1,0:T(8,128)(2,1)} %param.14), kind=kOutput, calls=%fused_computation.27 | convolution fusion | flops 2416508928 | bytes 7733248 | tf_op jit(solution)/shard_map/dot_general | solution.py:93
  61.6 2.6 fusion.11
  64.2 2.6 fusion.12
  68.3 80.9 %all_to_all.33 = bf16[2,576,3,1024]{3,1,2,0:T(8,128)(2,1)S(1)} all-to-all(bf16[2,576,3,1024]{3,1,2,0:T(8,128)(2,1)S(1)} %broadcast_in_dim.11), channel_id=1, replica_groups=mesh['dp'=32,'expert'=2,'tensor'=2] {'tensor'}, dimensions={0} | all-to-all | bytes 14155776 | tf_op jit(solution)/shard_map/all_to_all | solution.py:17
  149.2 1.9 convert_reduce_fusion
  153.5 3.5 convert_element_type.56
  156.9 12.2 %convolution_convert_fusion.1 = bf16[32,18,3,2048]{3,0,2,1:T(8,128)(2,1)S(1)} fusion(bf16[1024,2048]{1,0:T(8,128)(2,1)} %param.17, bf16[32,18,3,1024]{3,1,0,2:T(8,128)(2,1)} %convert_element_type.56), kind=kOutput, calls=%fused_computation.4 | convolution fusion | flops 7251296256 | bytes 14811136 | tf_op jit(solution)/shard_map/dot_general | solution.py:102
  169.1 7.3 %copy.153 = bf16[32,18,3,2048]{3,2,1,0:T(4,128)(2,1)} copy(bf16[32,18,3,2048]{3,0,2,1:T(8,128)(2,1)S(1)} %convolution_convert_fusion.1) | data formatting | bytes 14155776 | tf_op jit(solution)/shard_map/convert_element_type | solution.py:105
  176.4 5.8 %all-to-all-start.2 = ((bf16[32,18,3,2048]{3,2,1,0:T(4,128)(2,1)}), bf16[32,18,3,2048]{3,2,1,0:T(4,128)(2,1)}, u32[]{:S(2)}, u32[]{:S(2)}) async-start(bf16[32,18,3,2048]{3,2,1,0:T(4,128)(2,1)} %copy.153), calls=%async_computation.2 | async-start | bytes 18874368 | tf_op jit(solution)/shard_map/all_to_all | solution.py:106
  182.2 112.5 %all-to-all-done.2 = bf16[32,18,3,2048]{3,2,1,0:T(4,128)(2,1)} async-done(((bf16[32,18,3,2048]{3,2,1,0:T(4,128)(2,1)}), bf16[32,18,3,2048]{3,2,1,0:T(4,128)(2,1)}, u32[]{:S(2)}, u32[]{:S(2)}) %all-to-all-start.2) | async-done | bytes 7077920 | tf_op jit(solution)/shard_map/all_to_all | solution.py:106
  294.7 10.4 %bitcast_reduce_fusion = bf16[8,18,3,2048]{3,2,1,0:T(4,128)(2,1)S(1)} fusion(bf16[32,18,3,2048]{3,2,1,0:T(4,128)(2,1)} %all-to-all-done.2), kind=kLoop, calls=%fused_computation.1 | loop fusion | flops 2654208 | bytes 8847360 | tf_op jit(solution)/shard_map/reduce_sum | solution.py:107
  307.1 2.1 broadcast_in_dim.12
  309.2 5.6 %all-to-all-start.3 = ((bf16[2,128,6144]{2,1,0:T(8,128)(2,1)}), bf16[2,128,6144]{2,1,0:T(8,128)(2,1)}, u32[]{:S(2)}, u32[]{:S(2)}) async-start(bf16[2,128,6144]{2,1,0:T(8,128)(2,1)} %broadcast_in_dim.12), calls=%async_computation.3 | async-start | bytes 6291456 | tf_op jit(solution)/shard_map/all_to_all | solution.py:17
  314.9 30.2 %all-to-all-done.3 = bf16[2,128,6144]{2,1,0:T(8,128)(2,1)} async-done(((bf16[2,128,6144]{2,1,0:T(8,128)(2,1)}), bf16[2,128,6144]{2,1,0:T(8,128)(2,1)}, u32[]{:S(2)}, u32[]{:S(2)}) %all-to-all-start.3) | async-done | bytes 3145760 | tf_op jit(solution)/shard_map/all_to_all | solution.py:17
  345.1 2.8 convert_reduce_fusion.1
  347.9 3.8 reshape.173
  351.7 8.3 %fusion.41 = (f32[64,2,1,2048]{3,2,1,0:T(1,128)S(1)}, f32[64,2,1,2048]{3,2,1,0:T(1,128)S(1)}, f32[64,2,1,2048]{3,2,1,0:T(1,128)S(1)}) fusion(f32[64,2,3,2048]{3,2,1,0:T(4,128)} %reshape.173), kind=kLoop, calls=%fused_computation.117 | loop fusion | bytes 6291456 | tf_op jit(solution)/shard_map/slice | solution.py:115
  360.0 2.3 fusion.16
  362.7 5.0 %multiply_reduce_fusion.1 = (f32[64,2]{1,0:T(8,128)S(1)}, f32[64,2]{1,0:T(8,128)S(1)}, f32[64,2]{1,0:T(8,128)S(1)}, f32[64,2]{1,0:T(8,128)S(1)}, f32[64,2]{1,0:T...) fusion(f32[64,2048]{1,0:T(8,128)S(1)} %get-tuple-element.37, ...), kind=kLoop, calls=%fused_computation.38 | loop fusion | flops 4979712 | bytes 3682816 | tf_op jit(solution)/shard_map/reduce_sum | solution.py:127
  369.0 5.0 %all_to_all.34 = f32[2,1,1216]{2,1,0:T(1,128)S(1)} all-to-all(f32[2,1,1216]{2,1,0:T(1,128)S(1)} %broadcast_in_dim.13), channel_id=1, replica_groups=mesh['dp'=32,'expert'=2,'tensor'=2] {'tensor'}, dimensions={0} | all-to-all | bytes 19456 | tf_op jit(solution)/shard_map/all_to_all | solution.py:17
  377.5 16.9 %all-to-all-start.5 = ((f32[32,1,16]{2,1,0:T(1,128)}), f32[32,1,16]{2,1,0:T(1,128)S(1)}, u32[]{:S(2)}, u32[]{:S(2)}) async-start(f32[32,1,16]{2,1,0:T(1,128)} %broadcast_in_dim.14), calls=%async_computation.5 | async-start | bytes 32768 | tf_op jit(solution)/shard_map/all_to_all | solution.py:17
  395.0 6.4 %all-to-all-done.5 = f32[32,1,16]{2,1,0:T(1,128)S(1)} async-done(((f32[32,1,16]{2,1,0:T(1,128)}), f32[32,1,16]{2,1,0:T(1,128)S(1)}, u32[]{:S(2)}, u32[]{:S(2)}) %all-to-all-start.5) | async-done | bytes 2080 | tf_op jit(solution)/shard_map/all_to_all | solution.py:17
  (83 shorter events, 16.1 us)
Async XLA Ops:
  55.9 5.7 %copy-start = (bf16[576,2048]{1,0:T(8,128)(2,1)S(1)}, bf16[576,2048]{1,0:T(8,128)(2,1)}, u32[]{:S(2)}) copy-start(bf16[576,2048]{1,0:T(8,128)(2,1)} %reshape.170) | copy-start | bytes 7077892
  55.9 5.7 %copy-start.6 = (bf16[2048,1024]{1,0:T(8,128)(2,1)S(1)}, bf16[2048,1024]{1,0:T(8,128)(2,1)}, u32[]{:S(2)}) copy-start(bf16[2048,1024]{1,0:T(8,128)(2,1)} %param.15) | copy-start | bytes 12582916
  61.5 2.7 copy-start.7
  176.4 118.3 %all-to-all-start.2 = ((bf16[32,18,3,2048]{3,2,1,0:T(4,128)(2,1)}), bf16[32,18,3,2048]{3,2,1,0:T(4,128)(2,1)}, u32[]{:S(2)}, u32[]{:S(2)}) async-start(bf16[32,18,3,2048]{3,2,1,0:T(4,128)(2,1)} %copy.153), calls=%async_computation.2 | async-start | bytes 18874368 | tf_op jit(solution)/shard_map/all_to_all | solution.py:106
  309.2 5.6 %copy-start.5 = (f32[64,2]{0,1:T(2,128)S(1)}, f32[64,2]{0,1:T(2,128)}, u32[]{:S(2)}) copy-start(f32[64,2]{0,1:T(2,128)} %param.13) | copy-start | bytes 1540
  309.2 5.7 %copy-start.3 = (f32[2048]{0:T(1024)S(1)}, f32[2048]{0:T(1024)}, u32[]{:S(2)}) copy-start(f32[2048]{0:T(1024)} %param.11) | copy-start | bytes 24580
  309.2 35.9 %all-to-all-start.3 = ((bf16[2,128,6144]{2,1,0:T(8,128)(2,1)}), bf16[2,128,6144]{2,1,0:T(8,128)(2,1)}, u32[]{:S(2)}, u32[]{:S(2)}) async-start(bf16[2,128,6144]{2,1,0:T(8,128)(2,1)} %broadcast_in_dim.12), calls=%async_computation.3 | async-start | bytes 6291456 | tf_op jit(solution)/shard_map/all_to_all | solution.py:17
  351.7 10.6 %copy-start.1 = (bf16[64,2048]{1,0:T(8,128)(2,1)S(1)}, bf16[64,2048]{1,0:T(8,128)(2,1)}, u32[]{:S(2)}) copy-start(bf16[64,2048]{1,0:T(8,128)(2,1)} %param.9) | copy-start | bytes 786436
  360.0 2.4 copy-start.2
  367.7 9.0 %copy-start.4 = (s32[64,2]{0,1:T(2,128)S(1)}, s32[64,2]{0,1:T(2,128)}, u32[]{:S(2)}) copy-start(s32[64,2]{0,1:T(2,128)} %param.12) | copy-start | bytes 1540
  377.5 23.8 %all-to-all-start.5 = ((f32[32,1,16]{2,1,0:T(1,128)}), f32[32,1,16]{2,1,0:T(1,128)S(1)}, u32[]{:S(2)}, u32[]{:S(2)}) async-start(f32[32,1,16]{2,1,0:T(1,128)} %broadcast_in_dim.14), calls=%async_computation.5 | async-start | bytes 32768 | tf_op jit(solution)/shard_map/all_to_all | solution.py:17

commit v2 on v1

v2 whole, which is shorter than its diff:
```python
import functools

import jax
import jax.numpy as jnp
from jax import lax
from jax.experimental import pallas as pl
from jax.experimental.pallas import tpu as pltpu
from jax.sharding import PartitionSpec as P

D = 4096
EXPERTS = 8
TOK = 64
CAP = 18
MAIN = 16
FOLD = 8
PLANES = 4
OWNERS = 8
ROWS = OWNERS * CAP
WIDTH = 2048
PIECE = WIDTH // FOLD
BLOCK = WIDTH + PIECE
HIDDEN = 1024
HALF = HIDDEN // 2

epsilon = 1e-05
loss_weight = 8.0
bf16 = jnp.bfloat16
f32 = jnp.float32


def iota(shape, dim):
    return lax.broadcasted_iota(jnp.int32, shape, dim)


def ones_where(mask):
    return jnp.where(mask, 1.0, 0.0).astype(f32)


def dot(a, b):
    return jnp.dot(a, b, preferred_element_type=f32)


def slot_curvature(inv_root, moments, weighted_uu, resid_b, resid_a, resid_u):
    inv_cube = inv_root * inv_root * inv_root
    first_rate = 2.0 * moments[0] / D
    second_rate = 2.0 * (moments[1] + moments[2]) / D
    slope_one = -0.5 * inv_cube * first_rate
    slope_two = (
        0.75 * inv_cube * inv_root * inv_root * first_rate * first_rate
        - 0.5 * inv_cube * second_rate
    )
    tangent_sq = (
        inv_root * inv_root * moments[3]
        + 2.0 * inv_root * slope_one * moments[4]
        + slope_one * slope_one * weighted_uu
    )
    bending = inv_root * resid_b + 2.0 * slope_one * resid_a + slope_two * resid_u
    return 2.0 * loss_weight / D * (tangent_sq + bending)


def kernel(
    ids_ref, ids_row_ref, prob_ref, gain_ref, tokens_ref, targets_ref, wg_hbm, wp_hbm, wu_hbm, wd_hbm,
    normed_ref, curv_ref, est_ref,
    w_in, w_down, out_rows, rows, lhs, tsend, trecv, jets, folded, img, sib, ret,
    pown, prec, aown, asend, arec, bown, usum, stat, est_core, est_all,
    w_sem, d_send, d_recv, f_send, f_recv, t_send, t_recv, s_send, s_recv, r_send, r_recv,
    e_send, e_recv, st_send, st_recv, c_send, c_recv, a_send, a_recv,
):
    dp = lax.axis_index("dp")
    x_half = lax.axis_index("expert")
    part = lax.axis_index("tensor")
    z, y, core = dp // 8, (dp // 2) % 4, dp % 2
    chip = dp // 2
    sibling = {"dp": chip * 2 + (1 - core)}
    beside = {"tensor": 1 - part}
    across = {"expert": 1 - x_half}
    diagonal = {"expert": 1 - x_half, "tensor": 1 - part}

    def at(chip_index):
        return {"dp": chip_index * 2 + core}

    barrier = pltpu.get_barrier_semaphore()
    for who in (sibling, beside, across, diagonal):
        pl.semaphore_signal(barrier, inc=1, device_id=who)

    def greet(delta, _):
        pl.semaphore_signal(barrier, inc=1, device_id=at((chip + delta) % 16))
        return 0

    lax.fori_loop(1, 16, greet, 0)

    def weights(i):
        src = (wg_hbm, wp_hbm, wu_hbm)[i % 3].at[:, pl.ds((i // 3) * HALF, HALF)]
        return pltpu.make_async_copy(src, w_in.at[i], w_sem.at[i])

    for i in range(6):
        weights(i).start()
    down = pltpu.make_async_copy(wd_hbm, w_down, w_sem.at[6])
    down.start()

    ids = ids_ref[...]
    names = (ids[0:1, :] == iota((EXPERTS, TOK), 0)) | (ids[1:2, :] == iota((EXPERTS, TOK), 0))
    names = ones_where(names).astype(bf16)
    before = ones_where(iota((TOK, 2 * TOK), 0) < (iota((TOK, 2 * TOK), 1) & (TOK - 1))).astype(bf16)
    count = dot(names, before).astype(bf16)
    spread = ones_where((iota((128, EXPERTS), 0) >> 4) == iota((128, EXPERTS), 1)).astype(bf16)
    slot_of = dot(spread, count)[:, :TOK].astype(jnp.int32)
    named = dot(spread, names) > 0.5
    line = iota((128, TOK), 0)
    pick_main = ones_where(named & (slot_of == (line & 15))).astype(bf16)
    pick_fold = named & (slot_of == MAIN + (line & 1))
    out_rows[:, :, :WIDTH] = dot(pick_main, tokens_ref[...]).astype(bf16).reshape(EXPERTS, MAIN, WIDTH)
    fold = jnp.zeros((128, PIECE), f32)
    for f in range(FOLD):
        pick = ones_where(pick_fold & (((line >> 1) & 7) == f)).astype(bf16)
        fold = fold + dot(pick, tokens_ref[:, f * PIECE : (f + 1) * PIECE])
    out_rows[:, :, WIDTH:] = fold.astype(bf16).reshape(EXPERTS, MAIN, PIECE)

    pl.semaphore_wait(barrier, 19)

    def plane_of(j):
        return (z + (j + y) % PLANES) % PLANES

    def dispatch(j, q):
        target = plane_of(j) * 4 + q
        block = out_rows.at[plane_of(j) * 2 + q // 2]
        here = pltpu.make_async_copy(block, rows.at[j, core, y], d_recv.at[j, y])
        there = pltpu.make_async_remote_copy(
            src_ref=block, dst_ref=rows.at[j, core, y], send_sem=d_send.at[j, q], recv_sem=d_recv.at[j, y],
            device_id=at(target),
        )
        return target == chip, here, there

    def start_dispatch(j):
        def one(q, _):
            mine, here, there = dispatch(j, q)

            @pl.when(mine)
            def _():
                here.start()

            @pl.when(jnp.logical_not(mine))
            def _():
                there.start()

            return 0

        lax.fori_loop(0, 4, one, 0)

    def end_dispatch(j):
        def one(q, _):
            mine, _, there = dispatch(j, q)

            @pl.when(jnp.logical_not(mine))
            def _():
                there.wait_send()

            return 0

        lax.fori_loop(0, 4, one, 0)

    def passed_on(j):
        return pltpu.make_async_remote_copy(
            src_ref=rows.at[j, core], dst_ref=rows.at[j, core], send_sem=f_send.at[j], recv_sem=f_recv.at[j],
            device_id=sibling,
        )

    def arrive(j):
        def one(q, _):
            pltpu.make_async_copy(out_rows.at[0], rows.at[j, core, q], d_recv.at[j, q]).wait()
            return 0

        lax.fori_loop(0, 4, one, 0)
        passed_on(j).start()

    a_, b_ = iota((128, 128), 0), iota((128, 128), 1)
    swap = ones_where(
        ((a_ >> 4) == ((b_ >> 1) & 7)) & (((a_ >> 1) & 7) == (b_ >> 4)) & ((a_ & 1) == (b_ & 1))
    ).astype(bf16)

    def exchange(j, i):
        return pltpu.make_async_remote_copy(
            src_ref=tsend.at[j, i], dst_ref=trecv.at[j, i], send_sem=t_send.at[j, i], recv_sem=t_recv.at[j, i],
            device_id=beside,
        )

    def project(j, send):
        passed_on(j).wait_recv()
        lhs[: OWNERS * MAIN, :] = rows[j, :, :, :, :WIDTH].reshape(OWNERS * MAIN, WIDTH)
        extra = rows[j, :, :, :, WIDTH:].reshape(128, PIECE)
        extra = dot(swap, extra).astype(bf16)
        for f in range(FOLD):
            lhs[OWNERS * MAIN :, f * PIECE : (f + 1) * PIECE] = extra[f * 16 : (f + 1) * 16]

        def one(i, _):
            if j == 0:
                pltpu.make_async_copy(w_in.at[i], w_in.at[i], w_sem.at[i]).wait()
            tsend[j, i] = dot(lhs[...], w_in[i]).astype(bf16)
            if send:
                exchange(j, i).start()
            return 0

        lax.fori_loop(0, 6, one, 0)

    def to_sibling(j):
        return pltpu.make_async_remote_copy(
            src_ref=img.at[j, 1 - core], dst_ref=sib.at[j], send_sem=s_send.at[j], recv_sem=s_recv.at[j],
            device_id=sibling,
        )

    def expand(j):
        for half in range(2):
            for i in range(3):
                exchange(j, half * 3 + i).wait_recv()
            if j < PLANES - 1:
                for i in range(3):
                    exchange(j + 1, half * 3 + i).start()

            def one(block, _):
                at_ = pl.ds(pl.multiple_of(block * 16, 16), 16)

                def pre(i):
                    return tsend[j, half * 3 + i, at_].astype(f32) + trecv[j, half * 3 + i, at_].astype(f32)

                g, d, u = pre(0), pre(1), pre(2)
                s = jax.nn.sigmoid(g)
                first = s * (1.0 + g * (1.0 - s))
                second = s * (1.0 - s) * (2.0 + g * (1.0 - 2.0 * s))
                cols = slice(half * HALF, (half + 1) * HALF)
                jets[at_, cols] = (g * s * u).astype(bf16)
                jets[pl.ds(pl.multiple_of(ROWS + block * 16, 16), 16), cols] = (first * d * u).astype(bf16)
                jets[pl.ds(pl.multiple_of(2 * ROWS + block * 16, 16), 16), cols] = (second * d * d * u).astype(bf16)
                return 0

            lax.fori_loop(0, ROWS // 16, one, 0)
        if j == 0:
            down.wait()

        def piece(n, _):
            cols = pl.ds(pl.multiple_of(n * PIECE, PIECE), PIECE)
            out = dot(jets[...], w_down[:, cols]).astype(bf16)
            for i in range(3):
                top = i * ROWS
                img[j, :, :, i, :, cols] = out[top : top + 128].reshape(2, 4, MAIN, PIECE)
                folded[i, pl.ds(pl.multiple_of(n * 16, 16), 16)] = out[top + 128 : top + 144]
            return 0

        lax.fori_loop(0, FOLD, piece, 0)
        for i in range(3):
            extra = dot(swap, folded[i]).astype(bf16)
            img[j, :, :, i, :, WIDTH:] = extra.reshape(2, 4, MAIN, PIECE)
        to_sibling(j).start()

    def give(j, q):
        target = ((z + PLANES - (j + q) % PLANES) % PLANES) * 4 + q
        here = pltpu.make_async_copy(img.at[j, core, q], ret.at[j, y], r_recv.at[j, y])
        there = pltpu.make_async_remote_copy(
            src_ref=img.at[j, core, q], dst_ref=ret.at[j, y], send_sem=r_send.at[j, q], recv_sem=r_recv.at[j, y],
            device_id=at(target),
        )
        return target == chip, here, there

    def give_back(j):
        to_sibling(j).wait_recv()

        def one(q, _):
            img[j, core, q] = (img[j, core, q].astype(f32) + sib[j, q].astype(f32)).astype(bf16)
            mine, here, there = give(j, q)

            @pl.when(mine)
            def _():
                here.start()

            @pl.when(jnp.logical_not(mine))
            def _():
                there.start()

            return 0

        lax.fori_loop(0, 4, one, 0)

    start_dispatch(0)
    arrive(0)
    for j in range(1, PLANES):
        start_dispatch(j)
    project(0, True)
    arrive(1)
    project(1, False)
    arrive(2)
    arrive(3)
    expand(0)
    project(2, False)
    give_back(0)
    expand(1)
    project(3, False)
    give_back(1)
    expand(2)
    give_back(2)
    expand(3)

    ids_row = ids_row_ref[...]
    line = iota((256, 2 * TOK), 0)
    plane = (z + (((line >> 6) + y) & 3)) & 3
    expert_of = plane * 2 + ((line >> 5) & 1)
    small = iota((256, EXPERTS), 0)
    small = ((z + (((small >> 6) + y) & 3)) & 3) * 2 + ((small >> 5) & 1)
    spread_back = ones_where(small == iota((256, EXPERTS), 1)).astype(bf16)
    slot_back = dot(spread_back, count).astype(jnp.int32)
    mine = expert_of == ids_row
    back_main = ones_where(mine & (slot_back == (line & 15))).T.astype(bf16)
    back_fold = ones_where(mine & (slot_back == MAIN + (line & 1))).T
    fold_index = (iota((2 * TOK, 256), 1) >> 1) & 7
    eye = a_ == b_
    prob_col = jnp.sum(jnp.where(eye, prob_ref[...], 0.0), axis=1, keepdims=True)
    id_col = jnp.sum(jnp.where(eye, ids_row.astype(f32), 0.0), axis=1, keepdims=True)

    give_back(3)
    for j in range(PLANES):
        for q in range(4):
            pltpu.make_async_copy(ret.at[j, q], ret.at[j, q], r_recv.at[j, q]).wait()

    def pieces(f, _):
        cols = pl.ds(pl.multiple_of(f * PIECE, PIECE), PIECE)
        pick = jnp.where(fold_index == f, back_fold, 0.0).astype(bf16)

        def picked(i):
            whole = ret[:, :, i, :, cols].reshape(256, PIECE)
            extra = ret[:, :, i, :, WIDTH:].reshape(256, PIECE)
            return prob_col * (dot(back_main, whole) + dot(pick, extra))

        value = picked(0)
        pown[:, cols] = (value[:TOK] + value[TOK:]).astype(bf16)
        half_cols = pl.ds(pl.multiple_of((f % 4) * PIECE, PIECE), PIECE)
        tangent = picked(1)
        aown[f // 4, :, half_cols] = tangent
        asend[f // 4, :, half_cols] = tangent.astype(bf16)
        bown[:, cols] = picked(2)
        return 0

    lax.fori_loop(0, FOLD, pieces, 0)
    value_copy = pltpu.make_async_remote_copy(
        src_ref=pown, dst_ref=prec, send_sem=e_send.at[0], recv_sem=e_recv.at[0], device_id=across
    )
    tangent_copy = pltpu.make_async_remote_copy(
        src_ref=asend.at[1 - x_half], dst_ref=arec, send_sem=e_send.at[1], recv_sem=e_recv.at[1], device_id=across
    )
    value_copy.start()
    tangent_copy.start()
    value_copy.wait_recv()
    tangent_copy.wait_recv()

    me = x_half * 2 + part
    lane = iota((16, 128), 1)
    near = pl.ds(pl.multiple_of(x_half * (WIDTH // 2), WIDTH // 2), WIDTH // 2)

    def inner(block, _):
        at_ = pl.ds(pl.multiple_of(block * 16, 16), 16)
        u = tokens_ref[at_].astype(f32) + (pown[at_].astype(f32) + prec[at_].astype(f32))
        usum[at_] = u
        gain = gain_ref[...]
        heavy = gain * gain * u
        goal = gain * targets_ref[at_].astype(f32)
        stats = [None] * 19

        def over(v):
            return jnp.sum(v, axis=-1, keepdims=True)

        for k in range(2):
            b = bown[pl.ds(pl.multiple_of(k * TOK + block * 16, 16), 16)]
            stats[3 + k * 8 + 2] = over(u * b)
            stats[3 + k * 8 + 5] = over(heavy * b)
            stats[3 + k * 8 + 6] = over(goal * b)
        gain = gain_ref[:, near]
        u = usum[at_, near]
        heavy = gain * gain * u
        goal = gain * targets_ref[at_, near].astype(f32)
        stats[0] = over(u * u)
        stats[1] = over(heavy * u)
        stats[2] = over(goal * u)
        for k in range(2):
            own = pl.ds(pl.multiple_of(k * TOK + block * 16, 16), 16)
            a = aown[x_half, own] + arec[own].astype(f32)
            stats[3 + k * 8 + 0] = over(u * a)
            stats[3 + k * 8 + 1] = over(a * a)
            stats[3 + k * 8 + 3] = over(gain * gain * a * a)
            stats[3 + k * 8 + 4] = over(heavy * a)
            stats[3 + k * 8 + 7] = over(goal * a)
        laid = jnp.zeros((16, 128), f32)
        for i, value in enumerate(stats):
            laid = jnp.where(lane == i, value, laid)
        stat[me, at_] = laid
        return 0

    lax.fori_loop(0, TOK // 16, inner, 0)

    def stat_copy(i, who):
        return pltpu.make_async_remote_copy(
            src_ref=stat.at[me], dst_ref=stat.at[me], send_sem=st_send.at[i], recv_sem=st_recv.at[i], device_id=who
        )

    for i, who in enumerate((beside, across, diagonal)):
        stat_copy(i, who).start()
    for i, who in enumerate((beside, across, diagonal)):
        stat_copy(i, who).wait_recv()
    total = (stat[0] + stat[1]) + (stat[2] + stat[3])

    def column(i):
        return total[:, i : i + 1]

    inv_root = lax.rsqrt(column(0) / D + epsilon)
    weighted_uu = column(1)
    resid_u = inv_root * weighted_uu - column(2)
    sums = jnp.zeros((1, 128), f32)
    pairs = jnp.zeros((1, 128), f32)
    eye_tok = iota((TOK, TOK), 0) == iota((TOK, TOK), 1)
    for k in range(2):
        m = [column(3 + k * 8 + i) for i in range(8)]
        curve = slot_curvature(
            inv_root, m[:5], weighted_uu, inv_root * m[5] - m[6], inv_root * m[4] - m[7], resid_u
        )
        curv_ref[k : k + 1, :] = jnp.sum(jnp.where(eye_tok, curve, 0.0), axis=0, keepdims=True)
        member = ones_where(iota((TOK, 128), 1).astype(f32) == id_col[k * TOK : (k + 1) * TOK])
        sums = sums + jnp.sum(member * curve, axis=0, keepdims=True)
        pairs = pairs + jnp.sum(member, axis=0, keepdims=True)
    row = iota((8, 128), 0)
    est_core[core] = jnp.where(row == 0, sums, jnp.where(row == 1, pairs, 0.0))
    core_copy = pltpu.make_async_remote_copy(
        src_ref=est_core.at[core], dst_ref=est_core.at[core], send_sem=c_send, recv_sem=c_recv, device_id=sibling
    )
    core_copy.start()
    core_copy.wait_recv()
    est_all[chip] = est_core[0] + est_core[1]

    def all_copy(delta):
        return pltpu.make_async_remote_copy(
            src_ref=est_all.at[chip], dst_ref=est_all.at[chip], send_sem=a_send.at[delta], recv_sem=a_recv.at[delta],
            device_id=at((chip + delta) % 16),
        )

    def start_all(delta, _):
        all_copy(delta).start()
        return 0

    lax.fori_loop(1, 16, start_all, 0)
    for block in range(TOK // 16):
        at_ = slice(block * 16, (block + 1) * 16)
        normed_ref[at_] = (gain_ref[...] * usum[at_] * inv_root[at_]).astype(bf16)

    for j in range(PLANES):
        end_dispatch(j)
        passed_on(j).wait_send()
        for i in range(6):
            exchange(j, i).wait_send()
        to_sibling(j).wait_send()

        def gone(q, _):
            mine, _, there = give(j, q)

            @pl.when(jnp.logical_not(mine))
            def _():
                there.wait_send()

            return 0

        lax.fori_loop(0, 4, gone, 0)
    value_copy.wait_send()
    tangent_copy.wait_send()
    for i, who in enumerate((beside, across, diagonal)):
        stat_copy(i, who).wait_send()
    core_copy.wait_send()

    def end_all(delta, _):
        all_copy(delta).wait()
        return 0

    lax.fori_loop(1, 16, end_all, 0)
    final = jnp.sum(est_all[...], axis=0)
    est_ref[...] = final[0:1] / jnp.maximum(final[1:2], 1.0)


def on_device(tokens, targets, norm_gain, expert_ids, gate_prob, w_gate, gate_probe, w_up, w_down):
    vmem = pl.BlockSpec(memory_space=pltpu.VMEM)
    anywhere = pl.BlockSpec(memory_space=pl.ANY)
    dma = pltpu.SemaphoreType.DMA
    normed, curvature, estimate = pl.pallas_call(
        kernel,
        out_shape=(
            jax.ShapeDtypeStruct((TOK, WIDTH), bf16),
            jax.ShapeDtypeStruct((2, TOK), f32),
            jax.ShapeDtypeStruct((1, 128), f32),
        ),
        in_specs=[vmem] * 6 + [anywhere] * 4,
        out_specs=(vmem, vmem, vmem),
        scratch_shapes=[
            pltpu.VMEM((6, WIDTH, HALF), bf16),
            pltpu.VMEM((HIDDEN, WIDTH), bf16),
            pltpu.VMEM((EXPERTS, MAIN, BLOCK), bf16),
            pltpu.VMEM((PLANES, 2, 4, MAIN, BLOCK), bf16),
            pltpu.VMEM((ROWS, WIDTH), bf16),
            pltpu.VMEM((PLANES, 6, ROWS, HALF), bf16),
            pltpu.VMEM((PLANES, 6, ROWS, HALF), bf16),
            pltpu.VMEM((3 * ROWS, HIDDEN), bf16),
            pltpu.VMEM((3, 128, PIECE), bf16),
            pltpu.VMEM((PLANES, 2, 4, 3, MAIN, BLOCK), bf16),
            pltpu.VMEM((PLANES, 4, 3, MAIN, BLOCK), bf16),
            pltpu.VMEM((PLANES, 4, 3, MAIN, BLOCK), bf16),
            pltpu.VMEM((TOK, WIDTH), bf16),
            pltpu.VMEM((TOK, WIDTH), bf16),
            pltpu.VMEM((2, 2 * TOK, WIDTH // 2), f32),
            pltpu.VMEM((2, 2 * TOK, WIDTH // 2), bf16),
            pltpu.VMEM((2 * TOK, WIDTH // 2), bf16),
            pltpu.VMEM((2 * TOK, WIDTH), f32),
            pltpu.VMEM((TOK, WIDTH), f32),
            pltpu.VMEM((4, TOK, 128), f32),
            pltpu.VMEM((2, 8, 128), f32),
            pltpu.VMEM((16, 8, 128), f32),
            dma((7,)),
            dma((PLANES, 4)), dma((PLANES, 4)),
            dma((PLANES,)), dma((PLANES,)),
            dma((PLANES, 6)), dma((PLANES, 6)),
            dma((PLANES,)), dma((PLANES,)),
            dma((PLANES, 4)), dma((PLANES, 4)),
            dma((2,)), dma((2,)),
            dma((3,)), dma((3,)),
            dma, dma,
            dma((16,)), dma((16,)),
        ],
        compiler_params=pltpu.CompilerParams(
            collective_id=0, has_side_effects=True, vmem_limit_bytes=60 * 1024 * 1024
        ),
    )(
        expert_ids.T,
        expert_ids.T.reshape(1, 2 * TOK),
        gate_prob.T.reshape(1, 2 * TOK),
        norm_gain.reshape(1, WIDTH),
        tokens,
        targets,
        w_gate,
        gate_probe,
        w_up,
        w_down,
    )
    return normed, curvature.T, estimate[0, :EXPERTS]


def solution(mesh):
    return jax.shard_map(
        on_device,
        mesh=mesh,
        in_specs=(
            P("dp", "tensor"),
            P("dp", "tensor"),
            P("tensor"),
            P("dp", None),
            P("dp", None),
            P("tensor", ("dp", "expert")),
            P("tensor", ("dp", "expert")),
            P("tensor", ("dp", "expert")),
            P(("dp", "expert"), "tensor"),
        ),
        out_specs=(P("dp", "tensor"), P("dp", None), P()),
        check_vma=False,
    )
```

time: 403 us -> 158 us (0.39)
  Pallas kernels: 0 us -> 151 us
  waiting for transfers between devices: 149 us -> 0 us
  blocking collectives: 135 us -> 0 us
  other arithmetic: 29.1 us -> 0 us
  starting transfers between devices: 28.2 us -> 0 us
  local copies, waits for them, and re-layouts: 34.6 us -> 6.52 us
  matrix products: 25 us -> 0 us
    pallas_call x0 -> x1, Pallas kernels: none -> 151 us  [on_device(): pl.pallas_call(kernel, out_shape=(jax.ShapeDtypeStruct((TOK, WIDTH), bf16...]
    all_to_all x3 -> x0, waiting for transfers between devices: 149 us -> none  [the longest x1 113 us: on_device(): lax.all_to_all(images, 'dp', split_axis=0, concat_axis=0, tiled=True)]
    all_to_all x3 -> x0, blocking collectives: 135 us -> none  [the longest x2 85.9 us: sent_to_all(): return lax.all_to_all(copies, axis, split_axis=0, concat_axis=0, tiled=True)]
    all_to_all x3 -> x0, starting transfers between devices: 28.2 us -> none  [the longest x2 22.4 us: sent_to_all(): return lax.all_to_all(copies, axis, split_axis=0, concat_axis=0, tiled=True)]
    dot_general x6 -> x0, matrix products: 25 us -> none  [the longest x1 12.2 us: on_device(): jnp.dot(hidden_jets.reshape(-1, hidden_part), w_down, preferred_element_t...]
    reduce_sum x11 -> x0, other arithmetic: 23.2 us -> none  [the longest x1 10.4 us: on_device(): jnp.sum(returned.astype(jnp.float32).reshape(EXPERTS, holders, CAP, 3, wi...]
    convert_element_type x2 -> x0, local copies, waits for them, and re-layouts: 10.7 us -> none  [the longest x1 7.27 us: on_device(): images = images.reshape(senders, CAP, 3, width_part).astype(jnp.bfloat16)]
    slice x4 -> x0, local copies, waits for them, and re-layouts: 8.8 us -> none  [the longest x1 8.25 us: on_device(): tangent_out = weights * picked[:, :, 1]]
  transfers between devices with their start and end apart: 3 -> 0, of which waited for: 3 -> 0; matrix products, arithmetic and copies ran while one was open for 0% -> 0% of each run, Pallas kernels for 0% -> 0%
where the time goes in v2:
time: 158 us
  Pallas kernels  151 us (96%)
  local copies, waits for them, and re-layouts  6.52 us (4%)
    pallas_call x1, Pallas kernels, on_device(): pl.pallas_call(kernel, out_shape=(jax.ShapeDtypeStruct((TOK, WIDTH), bf16...  151 us

profile of v2, /device:TPU:1, one launch (start us, length us, event | category | flops | bytes accessed | tf_op | source)
XLA Modules:
  0.0 157.9 jit_solution(1735278535105600372)
XLA Ops:
  0.6 1.3 reshape.15.ids_row_ref
  1.9 1.3 reshape.16.prob_ref
  3.2 150.8 %shard_map.112 = (bf16[64,2048]{1,0:T(8,128)(2,1)}, f32[2,64]{1,0:T(2,128)}, f32[1,128]{1,0:T(1,128)}) custom-call(s32[2,64]{1,0:T(2,128)} %bitcast.8, s32[1,128]{1,0:T(1,128)} %reshape.15.ids_row_ref, f32[1,128]{1,0:T(1,128)} %reshape.16.prob_ref, f32[1,2048]{1,0:T(1,128)} %bitcast.6, bf16[64,2048]{1,0:T(8,128)(2,1)} %tokens_ref.1, ...), custom_call_target="tpu_custom_call" | custom-call | tf_op jit(solution)/shard_map/pallas_call | solution.py:485
  153.9 1.1 slice_bitcast_fusion
  155.0 1.7 %copy.14 = bf16[64,2048]{1,0:T(8,128)(2,1)} copy(bf16[64,2048]{1,0:T(8,128)(2,1)} %get-tuple-element.12) | data formatting | bytes 524288
  156.7 1.2 copy.15

commit v3 on v2

--- a/solution.py
+++ b/solution.py
@@ -21,6 +21,8 @@
 BLOCK = WIDTH + PIECE
 HIDDEN = 1024
 HALF = HIDDEN // 2
+OWN = (0, 64)
+OTHER = (64, 80)
 
 epsilon = 1e-05
 loss_weight = 8.0
@@ -59,8 +61,8 @@
 
 
 def kernel(
-    ids_ref, ids_row_ref, prob_ref, gain_ref, tokens_ref, targets_ref, wg_hbm, wp_hbm, wu_hbm, wd_hbm,
-    normed_ref, curv_ref, est_ref,
+    ids_ref, prob_ref, gain_ref, tokens_ref, targets_ref, wg_hbm, wp_hbm, wu_hbm, wd_hbm,
+    normed_ref, small_ref,
     w_in, w_down, out_rows, rows, lhs, tsend, trecv, jets, folded, img, sib, ret,
     pown, prec, aown, asend, arec, bown, usum, stat, est_core, est_all,
     w_sem, d_send, d_recv, f_send, f_recv, t_send, t_recv, s_send, s_recv, r_send, r_recv,
@@ -90,7 +92,7 @@
     lax.fori_loop(1, 16, greet, 0)
 
     def weights(i):
-        src = (wg_hbm, wp_hbm, wu_hbm)[i % 3].at[:, pl.ds((i // 3) * HALF, HALF)]
+        src = (wg_hbm, wp_hbm, wu_hbm)[i // 2].at[:, pl.ds((i % 2) * HALF, HALF)]
         return pltpu.make_async_copy(src, w_in.at[i], w_sem.at[i])
 
     for i in range(6):
@@ -101,10 +103,10 @@
     ids = ids_ref[...]
     names = (ids[0:1, :] == iota((EXPERTS, TOK), 0)) | (ids[1:2, :] == iota((EXPERTS, TOK), 0))
     names = ones_where(names).astype(bf16)
-    before = ones_where(iota((TOK, 2 * TOK), 0) < (iota((TOK, 2 * TOK), 1) & (TOK - 1))).astype(bf16)
+    before = ones_where(iota((TOK, TOK), 0) < iota((TOK, TOK), 1)).astype(bf16)
     count = dot(names, before).astype(bf16)
     spread = ones_where((iota((128, EXPERTS), 0) >> 4) == iota((128, EXPERTS), 1)).astype(bf16)
-    slot_of = dot(spread, count)[:, :TOK].astype(jnp.int32)
+    slot_of = dot(spread, count).astype(jnp.int32)
     named = dot(spread, names) > 0.5
     line = iota((128, TOK), 0)
     pick_main = ones_where(named & (slot_of == (line & 15))).astype(bf16)
@@ -178,29 +180,38 @@
         ((a_ >> 4) == ((b_ >> 1) & 7)) & (((a_ >> 1) & 7) == (b_ >> 4)) & ((a_ & 1) == (b_ & 1))
     ).astype(bf16)
 
-    def exchange(j, i):
+    def exchange(j, unit, i):
+        at_ = pl.ds(*unit)
+        number = 0 if unit == OWN else 1
         return pltpu.make_async_remote_copy(
-            src_ref=tsend.at[j, i], dst_ref=trecv.at[j, i], send_sem=t_send.at[j, i], recv_sem=t_recv.at[j, i],
-            device_id=beside,
-        )
-
-    def project(j, send):
-        passed_on(j).wait_recv()
-        lhs[: OWNERS * MAIN, :] = rows[j, :, :, :, :WIDTH].reshape(OWNERS * MAIN, WIDTH)
-        extra = rows[j, :, :, :, WIDTH:].reshape(128, PIECE)
-        extra = dot(swap, extra).astype(bf16)
-        for f in range(FOLD):
-            lhs[OWNERS * MAIN :, f * PIECE : (f + 1) * PIECE] = extra[f * 16 : (f + 1) * 16]
+            src_ref=tsend.at[j, i, at_], dst_ref=trecv.at[j, i, at_],
+            send_sem=t_send.at[j, number, i], recv_sem=t_recv.at[j, number, i], device_id=beside,
+        )
+
+    def project(j, unit, send):
+        first, many = unit
+        at_ = slice(first, first + many)
+        if unit == OWN:
+            lhs[at_, :] = rows[j, core, :, :, :WIDTH].reshape(64, WIDTH)
+        else:
+            passed_on(j).wait_recv()
+            lhs[64:128, :] = rows[j, 1 - core, :, :, :WIDTH].reshape(64, WIDTH)
+            extra = rows[j, :, :, :, WIDTH:].reshape(128, PIECE)
+            extra = dot(swap, extra).astype(bf16)
+            for f in range(FOLD):
+                lhs[128:, f * PIECE : (f + 1) * PIECE] = extra[f * 16 : (f + 1) * 16]
 
         def one(i, _):
-            if j == 0:
-                pltpu.make_async_copy(w_in.at[i], w_in.at[i], w_sem.at[i]).wait()
-            tsend[j, i] = dot(lhs[...], w_in[i]).astype(bf16)
+            for half in range(2):
+                w = i * 2 + half
+                if j == 0 and unit == OWN:
+                    pltpu.make_async_copy(w_in.at[w], w_in.at[w], w_sem.at[w]).wait()
+                tsend[j, i, at_, half * HALF : (half + 1) * HALF] = dot(lhs[at_, :], w_in[w]).astype(bf16)
             if send:
-                exchange(j, i).start()
-            return 0
-
-        lax.fori_loop(0, 6, one, 0)
+                exchange(j, unit, i).start()
+            return 0
+
+        lax.fori_loop(0, 3, one, 0)
 
     def to_sibling(j):
         return pltpu.make_async_remote_copy(
@@ -208,48 +219,50 @@
             device_id=sibling,
         )
 
-    def expand(j):
-        for half in range(2):
+    def expand(j, unit, following):
+        first, many = unit
+        for i in range(3):
+            exchange(j, unit, i).wait_recv()
+        if following:
             for i in range(3):
-                exchange(j, half * 3 + i).wait_recv()
-            if j < PLANES - 1:
-                for i in range(3):
-                    exchange(j + 1, half * 3 + i).start()
-
-            def one(block, _):
-                at_ = pl.ds(pl.multiple_of(block * 16, 16), 16)
-
-                def pre(i):
-                    return tsend[j, half * 3 + i, at_].astype(f32) + trecv[j, half * 3 + i, at_].astype(f32)
-
-                g, d, u = pre(0), pre(1), pre(2)
-                s = jax.nn.sigmoid(g)
-                first = s * (1.0 + g * (1.0 - s))
-                second = s * (1.0 - s) * (2.0 + g * (1.0 - 2.0 * s))
-                cols = slice(half * HALF, (half + 1) * HALF)
-                jets[at_, cols] = (g * s * u).astype(bf16)
-                jets[pl.ds(pl.multiple_of(ROWS + block * 16, 16), 16), cols] = (first * d * u).astype(bf16)
-                jets[pl.ds(pl.multiple_of(2 * ROWS + block * 16, 16), 16), cols] = (second * d * d * u).astype(bf16)
-                return 0
-
-            lax.fori_loop(0, ROWS // 16, one, 0)
-        if j == 0:
+                exchange(*following, i).start()
+
+        def one(block, _):
+            at_ = pl.ds(pl.multiple_of(first + block * 16, 16), 16)
+
+            def pre(i):
+                return tsend[j, i, at_].astype(f32) + trecv[j, i, at_].astype(f32)
+
+            g, d, u = pre(0), pre(1), pre(2)
+            s = jax.nn.sigmoid(g)
+            slope = s * (1.0 + g * (1.0 - s))
+            second = s * (1.0 - s) * (2.0 + g * (1.0 - 2.0 * s))
+            jets[pl.ds(pl.multiple_of(block * 16, 16), 16)] = (g * s * u).astype(bf16)
+            jets[pl.ds(pl.multiple_of(many + block * 16, 16), 16)] = (slope * d * u).astype(bf16)
+            jets[pl.ds(pl.multiple_of(2 * many + block * 16, 16), 16)] = (second * d * d * u).astype(bf16)
+            return 0
+
+        lax.fori_loop(0, many // 16, one, 0)
+        if j == 0 and unit == OWN:
             down.wait()
+        whose = core if unit == OWN else 1 - core
 
         def piece(n, _):
             cols = pl.ds(pl.multiple_of(n * PIECE, PIECE), PIECE)
-            out = dot(jets[...], w_down[:, cols]).astype(bf16)
+            out = dot(jets[: 3 * many], w_down[:, cols]).astype(bf16)
             for i in range(3):
-                top = i * ROWS
-                img[j, :, :, i, :, cols] = out[top : top + 128].reshape(2, 4, MAIN, PIECE)
-                folded[i, pl.ds(pl.multiple_of(n * 16, 16), 16)] = out[top + 128 : top + 144]
+                top = i * many
+                img[j, whose, :, i, :, cols] = out[top : top + 64].reshape(4, MAIN, PIECE)
+                if unit != OWN:
+                    folded[i, pl.ds(pl.multiple_of(n * 16, 16), 16)] = out[top + 64 : top + 80]
             return 0
 
         lax.fori_loop(0, FOLD, piece, 0)
-        for i in range(3):
-            extra = dot(swap, folded[i]).astype(bf16)
-            img[j, :, :, i, :, WIDTH:] = extra.reshape(2, 4, MAIN, PIECE)
-        to_sibling(j).start()
+        if unit != OWN:
+            for i in range(3):
+                extra = dot(swap, folded[i]).astype(bf16)
+                img[j, :, :, i, :, WIDTH:] = extra.reshape(2, 4, MAIN, PIECE)
+            to_sibling(j).start()
 
     def give(j, q):
         target = ((z + PLANES - (j + q) % PLANES) % PLANES) * 4 + q
@@ -279,92 +292,105 @@
 
         lax.fori_loop(0, 4, one, 0)
 
+    units = [(0, OWN), (0, OTHER)] + [(j, unit) for j in range(1, PLANES) for unit in (OTHER, OWN)]
     start_dispatch(0)
     arrive(0)
+    project(*units[0], True)
     for j in range(1, PLANES):
         start_dispatch(j)
-    project(0, True)
+    project(*units[1], True)
     arrive(1)
-    project(1, False)
+    project(*units[2], False)
     arrive(2)
     arrive(3)
-    expand(0)
-    project(2, False)
-    give_back(0)
-    expand(1)
-    project(3, False)
-    give_back(1)
-    expand(2)
-    give_back(2)
-    expand(3)
-
-    ids_row = ids_row_ref[...]
-    line = iota((256, 2 * TOK), 0)
+    for n, (j, unit) in enumerate(units):
+        expand(j, unit, units[n + 2] if n + 2 < len(units) else None)
+        if n + 3 < len(units):
+            project(*units[n + 3], False)
+        if n == 2:
+            give_back(0)
+        if j > 0 and unit == OWN:
+            give_back(j)
+
+    line = iota((256, TOK), 0)
     plane = (z + (((line >> 6) + y) & 3)) & 3
     expert_of = plane * 2 + ((line >> 5) & 1)
     small = iota((256, EXPERTS), 0)
     small = ((z + (((small >> 6) + y) & 3)) & 3) * 2 + ((small >> 5) & 1)
     spread_back = ones_where(small == iota((256, EXPERTS), 1)).astype(bf16)
     slot_back = dot(spread_back, count).astype(jnp.int32)
-    mine = expert_of == ids_row
-    back_main = ones_where(mine & (slot_back == (line & 15))).T.astype(bf16)
-    back_fold = ones_where(mine & (slot_back == MAIN + (line & 1))).T
+    eye_tok = iota((TOK, TOK), 0) == iota((TOK, TOK), 1)
+
+    def upright(row):
+        return jnp.sum(jnp.where(eye_tok, row, 0.0), axis=1, keepdims=True)
+
+    def for_ids(make):
+        return jnp.concatenate([make(ids[k : k + 1, :]) for k in range(2)], axis=0)
+
+    back_main = for_ids(lambda row: ones_where((expert_of == row) & (slot_back == (line & 15))).T).astype(bf16)
+    back_fold = for_ids(lambda row: ones_where((expert_of == row) & (slot_back == MAIN + (line & 1))).T)
     fold_index = (iota((2 * TOK, 256), 1) >> 1) & 7
-    eye = a_ == b_
-    prob_col = jnp.sum(jnp.where(eye, prob_ref[...], 0.0), axis=1, keepdims=True)
-    id_col = jnp.sum(jnp.where(eye, ids_row.astype(f32), 0.0), axis=1, keepdims=True)
-
-    give_back(3)
+    prob_col = jnp.concatenate([upright(prob_ref[k : k + 1, :]) for k in range(2)], axis=0)
+    id_col = [upright(ids[k : k + 1, :].astype(f32)) for k in range(2)]
+
     for j in range(PLANES):
         for q in range(4):
             pltpu.make_async_copy(ret.at[j, q], ret.at[j, q], r_recv.at[j, q]).wait()
 
-    def pieces(f, _):
-        cols = pl.ds(pl.multiple_of(f * PIECE, PIECE), PIECE)
+    def picked(i, f):
         pick = jnp.where(fold_index == f, back_fold, 0.0).astype(bf16)
-
-        def picked(i):
-            whole = ret[:, :, i, :, cols].reshape(256, PIECE)
-            extra = ret[:, :, i, :, WIDTH:].reshape(256, PIECE)
-            return prob_col * (dot(back_main, whole) + dot(pick, extra))
-
-        value = picked(0)
-        pown[:, cols] = (value[:TOK] + value[TOK:]).astype(bf16)
+        whole = ret[:, :, i, :, pl.ds(pl.multiple_of(f * PIECE, PIECE), PIECE)].reshape(256, PIECE)
+        extra = ret[:, :, i, :, WIDTH:].reshape(256, PIECE)
+        return prob_col * (dot(back_main, whole) + dot(pick, extra))
+
+    def values(f, _):
+        value = picked(0, f)
+        pown[:, pl.ds(pl.multiple_of(f * PIECE, PIECE), PIECE)] = (value[:TOK] + value[TOK:]).astype(bf16)
+        return 0
+
+    def tangents(f, _):
         half_cols = pl.ds(pl.multiple_of((f % 4) * PIECE, PIECE), PIECE)
-        tangent = picked(1)
+        tangent = picked(1, f)
         aown[f // 4, :, half_cols] = tangent
         asend[f // 4, :, half_cols] = tangent.astype(bf16)
-        bown[:, cols] = picked(2)
-        return 0
-
-    lax.fori_loop(0, FOLD, pieces, 0)
+        return 0
+
+    def seconds(f, _):
+        bown[:, pl.ds(pl.multiple_of(f * PIECE, PIECE), PIECE)] = picked(2, f)
+        return 0
+
     value_copy = pltpu.make_async_remote_copy(
         src_ref=pown, dst_ref=prec, send_sem=e_send.at[0], recv_sem=e_recv.at[0], device_id=across
     )
     tangent_copy = pltpu.make_async_remote_copy(
         src_ref=asend.at[1 - x_half], dst_ref=arec, send_sem=e_send.at[1], recv_sem=e_recv.at[1], device_id=across
     )
+    lax.fori_loop(0, FOLD, values, 0)
     value_copy.start()
+    lax.fori_loop(0, FOLD, tangents, 0)
     tangent_copy.start()
-    value_copy.wait_recv()
-    tangent_copy.wait_recv()
+    lax.fori_loop(0, FOLD, seconds, 0)
 
     me = x_half * 2 + part
     lane = iota((16, 128), 1)
     near = pl.ds(pl.multiple_of(x_half * (WIDTH // 2), WIDTH // 2), WIDTH // 2)
 
-    def inner(block, _):
+    def over(v):
+        return jnp.sum(v, axis=-1, keepdims=True)
+
+    def lay(values, laid):
+        for i, value in values.items():
+            laid = jnp.where(lane == i, value, laid)
+        return laid
+
+    def inner_value(block, _):
         at_ = pl.ds(pl.multiple_of(block * 16, 16), 16)
         u = tokens_ref[at_].astype(f32) + (pown[at_].astype(f32) + prec[at_].astype(f32))
         usum[at_] = u
         gain = gain_ref[...]
         heavy = gain * gain * u
         goal = gain * targets_ref[at_].astype(f32)
-        stats = [None] * 19
-
-        def over(v):
-            return jnp.sum(v, axis=-1, keepdims=True)
-
+        stats = {}
         for k in range(2):
             b = bown[pl.ds(pl.multiple_of(k * TOK + block * 16, 16), 16)]
             stats[3 + k * 8 + 2] = over(u * b)
@@ -377,6 +403,16 @@
         stats[0] = over(u * u)
         stats[1] = over(heavy * u)
         stats[2] = over(goal * u)
+        stat[me, at_] = lay(stats, jnp.zeros((16, 128), f32))
+        return 0
+
+    def inner_tangent(block, _):
+        at_ = pl.ds(pl.multiple_of(block * 16, 16), 16)
+        gain = gain_ref[:, near]
+        u = usum[at_, near]
+        heavy = gain * gain * u
+        goal = gain * targets_ref[at_, near].astype(f32)
+        stats = {}
         for k in range(2):
             own = pl.ds(pl.multiple_of(k * TOK + block * 16, 16), 16)
             a = aown[x_half, own] + arec[own].astype(f32)
@@ -385,13 +421,13 @@
             stats[3 + k * 8 + 3] = over(gain * gain * a * a)
             stats[3 + k * 8 + 4] = over(heavy * a)
             stats[3 + k * 8 + 7] = over(goal * a)
-        laid = jnp.zeros((16, 128), f32)
-        for i, value in enumerate(stats):
-            laid = jnp.where(lane == i, value, laid)
-        stat[me, at_] = laid
-        return 0
-
-    lax.fori_loop(0, TOK // 16, inner, 0)
+        stat[me, at_] = lay(stats, stat[me, at_])
+        return 0
+
+    value_copy.wait_recv()
+    lax.fori_loop(0, TOK // 16, inner_value, 0)
+    tangent_copy.wait_recv()
+    lax.fori_loop(0, TOK // 16, inner_tangent, 0)
 
     def stat_copy(i, who):
         return pltpu.make_async_remote_copy(
@@ -412,14 +448,14 @@
     resid_u = inv_root * weighted_uu - column(2)
     sums = jnp.zeros((1, 128), f32)
     pairs = jnp.zeros((1, 128), f32)
-    eye_tok = iota((TOK, TOK), 0) == iota((TOK, TOK), 1)
+    curves = []
     for k in range(2):
         m = [column(3 + k * 8 + i) for i in range(8)]
         curve = slot_curvature(
             inv_root, m[:5], weighted_uu, inv_root * m[5] - m[6], inv_root * m[4] - m[7], resid_u
         )
-        curv_ref[k : k + 1, :] = jnp.sum(jnp.where(eye_tok, curve, 0.0), axis=0, keepdims=True)
-        member = ones_where(iota((TOK, 128), 1).astype(f32) == id_col[k * TOK : (k + 1) * TOK])
+        curves.append(jnp.sum(jnp.where(eye_tok, curve, 0.0), axis=0, keepdims=True))
+        member = ones_where(iota((TOK, 128), 1).astype(f32) == id_col[k])
         sums = sums + jnp.sum(member * curve, axis=0, keepdims=True)
         pairs = pairs + jnp.sum(member, axis=0, keepdims=True)
     row = iota((8, 128), 0)
@@ -449,8 +485,9 @@
     for j in range(PLANES):
         end_dispatch(j)
         passed_on(j).wait_send()
-        for i in range(6):
-            exchange(j, i).wait_send()
+        for unit in (OWN, OTHER):
+            for i in range(3):
+                exchange(j, unit, i).wait_send()
         to_sibling(j).wait_send()
 
         def gone(q, _):
@@ -475,30 +512,36 @@
 
     lax.fori_loop(1, 16, end_all, 0)
     final = jnp.sum(est_all[...], axis=0)
-    est_ref[...] = final[0:1] / jnp.maximum(final[1:2], 1.0)
+    small_ref[0:2, 0:TOK] = jnp.concatenate(curves, axis=0)
+    small_ref[2:3, :] = final[0:1] / jnp.maximum(final[1:2], 1.0)
+
+
+def deliver(normed_in, small_in, normed_ref, curv_ref, est_ref):
+    normed_ref[...] = normed_in[...]
+    curv_ref[...] = small_in[0:2, 0:TOK]
+    est_ref[...] = small_in[2:3, 0:EXPERTS]
 
 
 def on_device(tokens, targets, norm_gain, expert_ids, gate_prob, w_gate, gate_probe, w_up, w_down):
     vmem = pl.BlockSpec(memory_space=pltpu.VMEM)
     anywhere = pl.BlockSpec(memory_space=pl.ANY)
     dma = pltpu.SemaphoreType.DMA
-    normed, curvature, estimate = pl.pallas_call(
+    normed, small = pl.pallas_call(
         kernel,
         out_shape=(
             jax.ShapeDtypeStruct((TOK, WIDTH), bf16),
-            jax.ShapeDtypeStruct((2, TOK), f32),
-            jax.ShapeDtypeStruct((1, 128), f32),
+            jax.ShapeDtypeStruct((8, 128), f32),
         ),
-        in_specs=[vmem] * 6 + [anywhere] * 4,
-        out_specs=(vmem, vmem, vmem),
+        in_specs=[vmem] * 5 + [anywhere] * 4,
+        out_specs=(vmem, vmem),
         scratch_shapes=[
             pltpu.VMEM((6, WIDTH, HALF), bf16),
             pltpu.VMEM((HIDDEN, WIDTH), bf16),
             pltpu.VMEM((EXPERTS, MAIN, BLOCK), bf16),
             pltpu.VMEM((PLANES, 2, 4, MAIN, BLOCK), bf16),
             pltpu.VMEM((ROWS, WIDTH), bf16),
-            pltpu.VMEM((PLANES, 6, ROWS, HALF), bf16),
-            pltpu.VMEM((PLANES, 6, ROWS, HALF), bf16),
+            pltpu.VMEM((PLANES, 3, ROWS, HIDDEN), bf16),
+            pltpu.VMEM((PLANES, 3, ROWS, HIDDEN), bf16),
             pltpu.VMEM((3 * ROWS, HIDDEN), bf16),
             pltpu.VMEM((3, 128, PIECE), bf16),
             pltpu.VMEM((PLANES, 2, 4, 3, MAIN, BLOCK), bf16),
@@ -517,7 +560,7 @@
             dma((7,)),
             dma((PLANES, 4)), dma((PLANES, 4)),
             dma((PLANES,)), dma((PLANES,)),
-            dma((PLANES, 6)), dma((PLANES, 6)),
+            dma((PLANES, 2, 3)), dma((PLANES, 2, 3)),
             dma((PLANES,)), dma((PLANES,)),
             dma((PLANES, 4)), dma((PLANES, 4)),
             dma((2,)), dma((2,)),
@@ -530,8 +573,7 @@
         ),
     )(
         expert_ids.T,
-        expert_ids.T.reshape(1, 2 * TOK),
-        gate_prob.T.reshape(1, 2 * TOK),
+        gate_prob.T,
         norm_gain.reshape(1, WIDTH),
         tokens,
         targets,
@@ -540,7 +582,17 @@
         w_up,
         w_down,
     )
-    return normed, curvature.T, estimate[0, :EXPERTS]
+    normed, curvature, estimate = pl.pallas_call(
+        deliver,
+        out_shape=(
+            jax.ShapeDtypeStruct((TOK, WIDTH), bf16),
+            jax.ShapeDtypeStruct((2, TOK), f32),
+            jax.ShapeDtypeStruct((1, EXPERTS), f32),
+        ),
+        in_specs=[vmem, vmem],
+        out_specs=(vmem, vmem, vmem),
+    )(normed, small)
+    return normed, curvature.T, estimate.reshape(EXPERTS)
 
 
 def solution(mesh):

time: 158 us -> 145 us (0.918)
  Pallas kernels: 151 us -> 144 us
  local copies, waits for them, and re-layouts: 6.52 us -> 0 us
    pallas_call x1, Pallas kernels: 151 us -> 143 us  [on_device(): pl.pallas_call(kernel, out_shape=(jax.ShapeDtypeStruct((TOK, WIDTH), bf16...]
    unnamed x2 -> x0, local copies, waits for them, and re-layouts: 2.9 us -> none
    reshape x2 -> x0, local copies, waits for them, and re-layouts: 2.54 us -> none  [the longest x1 1.27 us: on_device(): expert_ids.T.reshape(1, 2 * TOK)]
    pallas_call x0 -> x1, Pallas kernels: none -> 1.68 us  [on_device(): pl.pallas_call(deliver, out_shape=(jax.ShapeDtypeStruct((TOK, WIDTH), bf1...]
where the time goes in v3:
time: 145 us
  Pallas kernels  144 us (99%)
    pallas_call x1, Pallas kernels, on_device(): pl.pallas_call(kernel, out_shape=(jax.ShapeDtypeStruct((TOK, WIDTH), bf16...  143 us

profile of v3, /device:TPU:1, one launch (start us, length us, event | category | flops | bytes accessed | tf_op | source)
XLA Modules:
  0.0 145.1 jit_solution(14071170722204840452)
XLA Ops:
  0.6 142.7 %shard_map.112 = (bf16[64,2048]{1,0:T(8,128)(2,1)}, f32[8,128]{1,0:T(8,128)}) custom-call(s32[2,64]{1,0:T(2,128)} %bitcast.6, f32[2,64]{1,0:T(2,128)} %bitcast.7, f32[1,2048]{1,0:T(1,128)} %bitcast.5, bf16[64,2048]{1,0:T(8,128)(2,1)} %tokens_ref.1, bf16[64,2048]{1,0:T(8,128)(2,1)} %targets_ref.1, bf16[2048,1024]{1,0:T(8,128)(2,1)} %wg_hbm.1, ...), custom_call_target="tpu_custom_call" | custom-call | tf_op jit(solution)/shard_map/pallas_call | solution.py:529
  143.4 1.7 %shard_map.113 = (bf16[64,2048]{1,0:T(8,128)(2,1)}, f32[2,64]{1,0:T(2,128)}, f32[1,8]{1,0:T(1,128)}) custom-call(bf16[64,2048]{1,0:T(8,128)(2,1)} %get-tuple-element.8.normed_in, f32[8,128]{1,0:T(8,128)} %get-tuple-element.9.small_in), custom_call_target="tpu_custom_call" | custom-call | tf_op jit(solution)/shard_map/pallas_call | solution.py:585

commit v4 on v3

--- a/solution.py
+++ b/solution.py
@@ -120,12 +120,12 @@
 
     pl.semaphore_wait(barrier, 19)
 
-    def plane_of(j):
-        return (z + (j + y) % PLANES) % PLANES
+    def plane_of(j, q):
+        return (z + (j + y + q) % PLANES) % PLANES
 
     def dispatch(j, q):
-        target = plane_of(j) * 4 + q
-        block = out_rows.at[plane_of(j) * 2 + q // 2]
+        target = plane_of(j, q) * 4 + q
+        block = out_rows.at[plane_of(j, q) * 2 + q // 2]
         here = pltpu.make_async_copy(block, rows.at[j, core, y], d_recv.at[j, y])
         there = pltpu.make_async_remote_copy(
             src_ref=block, dst_ref=rows.at[j, core, y], send_sem=d_send.at[j, q], recv_sem=d_recv.at[j, y],
@@ -265,7 +265,7 @@
             to_sibling(j).start()
 
     def give(j, q):
-        target = ((z + PLANES - (j + q) % PLANES) % PLANES) * 4 + q
+        target = ((z + PLANES - (j + y + q) % PLANES) % PLANES) * 4 + q
         here = pltpu.make_async_copy(img.at[j, core, q], ret.at[j, y], r_recv.at[j, y])
         there = pltpu.make_async_remote_copy(
             src_ref=img.at[j, core, q], dst_ref=ret.at[j, y], send_sem=r_send.at[j, q], recv_sem=r_recv.at[j, y],
@@ -313,10 +313,10 @@
             give_back(j)
 
     line = iota((256, TOK), 0)
-    plane = (z + (((line >> 6) + y) & 3)) & 3
+    plane = (z + (((line >> 6) + (line >> 4) + y) & 3)) & 3
     expert_of = plane * 2 + ((line >> 5) & 1)
     small = iota((256, EXPERTS), 0)
-    small = ((z + (((small >> 6) + y) & 3)) & 3) * 2 + ((small >> 5) & 1)
+    small = ((z + (((small >> 6) + (small >> 4) + y) & 3)) & 3) * 2 + ((small >> 5) & 1)
     spread_back = ones_where(small == iota((256, EXPERTS), 1)).astype(bf16)
     slot_back = dot(spread_back, count).astype(jnp.int32)
     eye_tok = iota((TOK, TOK), 0) == iota((TOK, TOK), 1)

time: 145 us -> 136 us (0.938)
  Pallas kernels: 144 us -> 136 us
    pallas_call x1, Pallas kernels: 143 us -> 134 us  [on_device(): pl.pallas_call(kernel, out_shape=(jax.ShapeDtypeStruct((TOK, WIDTH), bf16...]
where the time goes in v4:
time: 136 us
  Pallas kernels  136 us (100%)
    pallas_call x1, Pallas kernels, on_device(): pl.pallas_call(kernel, out_shape=(jax.ShapeDtypeStruct((TOK, WIDTH), bf16...  134 us

profile of v4, /device:TPU:1, one launch (start us, length us, event | category | flops | bytes accessed | tf_op | source)
XLA Modules:
  0.0 136.3 jit_solution(12804618443785746985)
XLA Ops:
  0.6 134.0 %shard_map.112 = (bf16[64,2048]{1,0:T(8,128)(2,1)}, f32[8,128]{1,0:T(8,128)}) custom-call(s32[2,64]{1,0:T(2,128)} %bitcast.6, f32[2,64]{1,0:T(2,128)} %bitcast.7, f32[1,2048]{1,0:T(1,128)} %bitcast.5, bf16[64,2048]{1,0:T(8,128)(2,1)} %tokens_ref.1, bf16[64,2048]{1,0:T(8,128)(2,1)} %targets_ref.1, bf16[2048,1024]{1,0:T(8,128)(2,1)} %wg_hbm.1, ...), custom_call_target="tpu_custom_call" | custom-call | tf_op jit(solution)/shard_map/pallas_call | solution.py:529
  134.6 1.7 %shard_map.113 = (bf16[64,2048]{1,0:T(8,128)(2,1)}, f32[2,64]{1,0:T(2,128)}, f32[1,8]{1,0:T(1,128)}) custom-call(bf16[64,2048]{1,0:T(8,128)(2,1)} %get-tuple-element.8.normed_in, f32[8,128]{1,0:T(8,128)} %get-tuple-element.9.small_in), custom_call_target="tpu_custom_call" | custom-call | tf_op jit(solution)/shard_map/pallas_call | solution.py:585

commit v5 on v4

--- a/solution.py
+++ b/solution.py
@@ -23,6 +23,9 @@
 HALF = HIDDEN // 2
 OWN = (0, 64)
 OTHER = (64, 80)
+OWN_A = (0, 32)
+OWN_B = (32, 32)
+UNITS = [(0, OWN), (0, OTHER), (1, OTHER), (1, OWN), (2, OTHER), (2, OWN), (3, OTHER), (3, OWN_A), (3, OWN_B)]
 
 epsilon = 1e-05
 loss_weight = 8.0
@@ -64,7 +67,7 @@
     ids_ref, prob_ref, gain_ref, tokens_ref, targets_ref, wg_hbm, wp_hbm, wu_hbm, wd_hbm,
     normed_ref, small_ref,
     w_in, w_down, out_rows, rows, lhs, tsend, trecv, jets, folded, img, sib, ret,
-    pown, prec, aown, asend, arec, bown, usum, stat, est_core, est_all,
+    pown, prec, aown, asend, arec, bown, usum, slot_value, slot_tangent, tangent_out, stat, est_core, est_all,
     w_sem, d_send, d_recv, f_send, f_recv, t_send, t_recv, s_send, s_recv, r_send, r_recv,
     e_send, e_recv, st_send, st_recv, c_send, c_recv, a_send, a_recv,
 ):
@@ -121,7 +124,7 @@
     pl.semaphore_wait(barrier, 19)
 
     def plane_of(j, q):
-        return (z + (j + y + q) % PLANES) % PLANES
+        return (z + (j + y + 2 * (q // 2)) % PLANES) % PLANES
 
     def dispatch(j, q):
         target = plane_of(j, q) * 4 + q
@@ -182,7 +185,7 @@
 
     def exchange(j, unit, i):
         at_ = pl.ds(*unit)
-        number = 0 if unit == OWN else 1
+        number = {OWN: 0, OTHER: 1, OWN_A: 0, OWN_B: 2}[unit]
         return pltpu.make_async_remote_copy(
             src_ref=tsend.at[j, i, at_], dst_ref=trecv.at[j, i, at_],
             send_sem=t_send.at[j, number, i], recv_sem=t_recv.at[j, number, i], device_id=beside,
@@ -191,8 +194,8 @@
     def project(j, unit, send):
         first, many = unit
         at_ = slice(first, first + many)
-        if unit == OWN:
-            lhs[at_, :] = rows[j, core, :, :, :WIDTH].reshape(64, WIDTH)
+        if unit != OTHER:
+            lhs[at_, :] = rows[j, core, first // 16 : (first + many) // 16, :, :WIDTH].reshape(many, WIDTH)
         else:
             passed_on(j).wait_recv()
             lhs[64:128, :] = rows[j, 1 - core, :, :, :WIDTH].reshape(64, WIDTH)
@@ -219,13 +222,15 @@
             device_id=sibling,
         )
 
-    def expand(j, unit, following):
+    def expand(j, unit, following, then=None):
         first, many = unit
         for i in range(3):
             exchange(j, unit, i).wait_recv()
         if following:
             for i in range(3):
                 exchange(*following, i).start()
+        if then:
+            then()
 
         def one(block, _):
             at_ = pl.ds(pl.multiple_of(first + block * 16, 16), 16)
@@ -245,27 +250,29 @@
         lax.fori_loop(0, many // 16, one, 0)
         if j == 0 and unit == OWN:
             down.wait()
-        whose = core if unit == OWN else 1 - core
+        whose = 1 - core if unit == OTHER else core
+        places = slice(0, 4) if unit == OTHER else slice(first // 16, (first + many) // 16)
+        whole = 64 if unit == OTHER else many
 
         def piece(n, _):
             cols = pl.ds(pl.multiple_of(n * PIECE, PIECE), PIECE)
             out = dot(jets[: 3 * many], w_down[:, cols]).astype(bf16)
             for i in range(3):
                 top = i * many
-                img[j, whose, :, i, :, cols] = out[top : top + 64].reshape(4, MAIN, PIECE)
-                if unit != OWN:
+                img[j, whose, places, i, :, cols] = out[top : top + whole].reshape(whole // 16, MAIN, PIECE)
+                if unit == OTHER:
                     folded[i, pl.ds(pl.multiple_of(n * 16, 16), 16)] = out[top + 64 : top + 80]
             return 0
 
         lax.fori_loop(0, FOLD, piece, 0)
-        if unit != OWN:
+        if unit == OTHER:
             for i in range(3):
                 extra = dot(swap, folded[i]).astype(bf16)
                 img[j, :, :, i, :, WIDTH:] = extra.reshape(2, 4, MAIN, PIECE)
             to_sibling(j).start()
 
     def give(j, q):
-        target = ((z + PLANES - (j + y + q) % PLANES) % PLANES) * 4 + q
+        target = ((z + PLANES - (j + q + 2 * (y // 2)) % PLANES) % PLANES) * 4 + q
         here = pltpu.make_async_copy(img.at[j, core, q], ret.at[j, y], r_recv.at[j, y])
         there = pltpu.make_async_remote_copy(
             src_ref=img.at[j, core, q], dst_ref=ret.at[j, y], send_sem=r_send.at[j, q], recv_sem=r_recv.at[j, y],
@@ -273,8 +280,9 @@
         )
         return target == chip, here, there
 
-    def give_back(j):
-        to_sibling(j).wait_recv()
+    def give_back(j, low=0, high=4):
+        if low == 0:
+            to_sibling(j).wait_recv()
 
         def one(q, _):
             img[j, core, q] = (img[j, core, q].astype(f32) + sib[j, q].astype(f32)).astype(bf16)
@@ -290,90 +298,160 @@
 
             return 0
 
-        lax.fori_loop(0, 4, one, 0)
-
-    units = [(0, OWN), (0, OTHER)] + [(j, unit) for j in range(1, PLANES) for unit in (OTHER, OWN)]
+        lax.fori_loop(low, high, one, 0)
+
+    eye_tok = iota((TOK, TOK), 0) == iota((TOK, TOK), 1)
+
+    def upright(row):
+        return jnp.sum(jnp.where(eye_tok, row, 0.0), axis=1, keepdims=True)
+
+    prob_col = jnp.concatenate([upright(prob_ref[k : k + 1, :]) for k in range(2)], axis=0)
+    id_col = [upright(ids[k : k + 1, :].astype(f32)) for k in range(2)]
+
+    def back(many, place):
+        line = iota((many, TOK), 0)
+
+        def expert(line):
+            j, pair = place(line)
+            return ((z + ((j + y + 2 * pair) & 3)) & 3) * 2 + pair
+
+        spread = ones_where(expert(iota((many, EXPERTS), 0)) == iota((many, EXPERTS), 1)).astype(bf16)
+        slot = dot(spread, count).astype(jnp.int32)
+
+        def for_ids(wanted):
+            masks = [(expert(line) == ids[k : k + 1, :]) & (slot == wanted) for k in range(2)]
+            return jnp.concatenate([ones_where(m).T for m in masks], axis=0)
+
+        return for_ids(line & 15).astype(bf16), for_ids(MAIN + (line & 1)), (iota((2 * TOK, many), 1) >> 1) & 7
+
+    def picked(backs, whole, extra, f):
+        main, fold, index = backs
+        pick = jnp.where(index == f, fold, 0.0).astype(bf16)
+        return prob_col * (dot(main, whole) + dot(pick, extra))
+
+    def across_copy(i, src, dst):
+        return pltpu.make_async_remote_copy(
+            src_ref=src, dst_ref=dst, send_sem=e_send.at[i], recv_sem=e_recv.at[i], device_id=across
+        )
+
+    def early_value():
+        return across_copy(0, pown, prec)
+
+    def early_tangent():
+        return across_copy(1, asend.at[1 - x_half], arec)
+
+    def late_value():
+        return across_copy(2, slot_value.at[x_half], slot_value.at[x_half])
+
+    def late_tangent():
+        return across_copy(3, tangent_out, slot_tangent.at[x_half])
+
+    def returned(j):
+        for q in range(4):
+            pltpu.make_async_copy(ret.at[j, q], ret.at[j, q], r_recv.at[j, q]).wait()
+
+    def early():
+        backs = back(64 * (PLANES - 1), lambda line: (line >> 6, (line >> 5) & 1))
+        for j in range(PLANES - 1):
+            returned(j)
+
+        def piece(f, _):
+            cols = pl.ds(pl.multiple_of(f * PIECE, PIECE), PIECE)
+            half_cols = pl.ds(pl.multiple_of((f % 4) * PIECE, PIECE), PIECE)
+
+            def of(i):
+                whole = ret[: PLANES - 1, :, i, :, cols].reshape(64 * (PLANES - 1), PIECE)
+                extra = ret[: PLANES - 1, :, i, :, WIDTH:].reshape(64 * (PLANES - 1), PIECE)
+                return picked(backs, whole, extra, f)
+
+            value = of(0)
+            pown[:, cols] = (value[:TOK] + value[TOK:]).astype(bf16)
+            tangent = of(1)
+            aown[f // 4, :, half_cols] = tangent
+            asend[f // 4, :, half_cols] = tangent.astype(bf16)
+            bown[:, cols] = of(2)
+            return 0
+
+        lax.fori_loop(0, FOLD, piece, 0)
+
+    def send_early():
+        early_value().start()
+        early_tangent().start()
+
     start_dispatch(0)
     arrive(0)
-    project(*units[0], True)
+    project(*UNITS[0], True)
     for j in range(1, PLANES):
         start_dispatch(j)
-    project(*units[1], True)
+    project(*UNITS[1], True)
     arrive(1)
-    project(*units[2], False)
+    project(*UNITS[2], False)
     arrive(2)
     arrive(3)
-    for n, (j, unit) in enumerate(units):
-        expand(j, unit, units[n + 2] if n + 2 < len(units) else None)
-        if n + 3 < len(units):
-            project(*units[n + 3], False)
+    for n, (j, unit) in enumerate(UNITS):
+        last = n == len(UNITS) - 1
+        expand(j, unit, UNITS[n + 2] if n + 2 < len(UNITS) else None, send_early if last else None)
+        if n + 3 < len(UNITS):
+            project(*UNITS[n + 3], False)
         if n == 2:
             give_back(0)
         if j > 0 and unit == OWN:
             give_back(j)
-
-    line = iota((256, TOK), 0)
-    plane = (z + (((line >> 6) + (line >> 4) + y) & 3)) & 3
-    expert_of = plane * 2 + ((line >> 5) & 1)
-    small = iota((256, EXPERTS), 0)
-    small = ((z + (((small >> 6) + (small >> 4) + y) & 3)) & 3) * 2 + ((small >> 5) & 1)
-    spread_back = ones_where(small == iota((256, EXPERTS), 1)).astype(bf16)
-    slot_back = dot(spread_back, count).astype(jnp.int32)
-    eye_tok = iota((TOK, TOK), 0) == iota((TOK, TOK), 1)
-
-    def upright(row):
-        return jnp.sum(jnp.where(eye_tok, row, 0.0), axis=1, keepdims=True)
-
-    def for_ids(make):
-        return jnp.concatenate([make(ids[k : k + 1, :]) for k in range(2)], axis=0)
-
-    back_main = for_ids(lambda row: ones_where((expert_of == row) & (slot_back == (line & 15))).T).astype(bf16)
-    back_fold = for_ids(lambda row: ones_where((expert_of == row) & (slot_back == MAIN + (line & 1))).T)
-    fold_index = (iota((2 * TOK, 256), 1) >> 1) & 7
-    prob_col = jnp.concatenate([upright(prob_ref[k : k + 1, :]) for k in range(2)], axis=0)
-    id_col = [upright(ids[k : k + 1, :].astype(f32)) for k in range(2)]
-
-    for j in range(PLANES):
-        for q in range(4):
-            pltpu.make_async_copy(ret.at[j, q], ret.at[j, q], r_recv.at[j, q]).wait()
-
-    def picked(i, f):
-        pick = jnp.where(fold_index == f, back_fold, 0.0).astype(bf16)
-        whole = ret[:, :, i, :, pl.ds(pl.multiple_of(f * PIECE, PIECE), PIECE)].reshape(256, PIECE)
-        extra = ret[:, :, i, :, WIDTH:].reshape(256, PIECE)
-        return prob_col * (dot(back_main, whole) + dot(pick, extra))
-
-    def values(f, _):
-        value = picked(0, f)
-        pown[:, pl.ds(pl.multiple_of(f * PIECE, PIECE), PIECE)] = (value[:TOK] + value[TOK:]).astype(bf16)
+        if unit == OWN_A:
+            give_back(j, 0, 2)
+        if unit == OWN_B:
+            give_back(j, 2, 4)
+        if (j, unit) == (3, OTHER):
+            early()
+
+    final = PLANES - 1
+    near = pl.ds(pl.multiple_of(x_half * (WIDTH // 2), WIDTH // 2), WIDTH // 2)
+    far = pl.ds(pl.multiple_of((1 - x_half) * (WIDTH // 2), WIDTH // 2), WIDTH // 2)
+    late_backs = back(64, lambda line: (final, (line >> 4) & 1))
+    second_backs = back(64, lambda line: (final, (line >> 5) & 1))
+    returned(final)
+
+    def pair_sum(pair, i, cols):
+        both = ret[final, 2 * pair, i, :, cols].astype(f32) + ret[final, 2 * pair + 1, i, :, cols].astype(f32)
+        return both.astype(bf16)
+
+    for pair in range(2):
+        slot_value[x_half, pair] = pair_sum(pair, 0, slice(0, BLOCK))
+    late_value().start()
+    for pair in range(2):
+        tangent_out[pair, :, : WIDTH // 2] = pair_sum(pair, 1, far)
+        tangent_out[pair, :, WIDTH // 2 :] = pair_sum(pair, 1, slice(WIDTH, BLOCK))
+    late_tangent().start()
+    for pair in range(2):
+        slot_tangent[x_half, pair, :, : WIDTH // 2] = pair_sum(pair, 1, near)
+        slot_tangent[x_half, pair, :, WIDTH // 2 :] = pair_sum(pair, 1, slice(WIDTH, BLOCK))
+
+    def late_second(f, _):
+        cols = pl.ds(pl.multiple_of(f * PIECE, PIECE), PIECE)
+        whole = ret[final, :, 2, :, cols].reshape(64, PIECE)
+        extra = ret[final, :, 2, :, WIDTH:].reshape(64, PIECE)
+        bown[:, cols] += picked(second_backs, whole, extra, f)
         return 0
 
-    def tangents(f, _):
-        half_cols = pl.ds(pl.multiple_of((f % 4) * PIECE, PIECE), PIECE)
-        tangent = picked(1, f)
-        aown[f // 4, :, half_cols] = tangent
-        asend[f // 4, :, half_cols] = tangent.astype(bf16)
+    lax.fori_loop(0, FOLD, late_second, 0)
+
+    def late_piece(f, _):
+        cols = pl.ds(pl.multiple_of(f * PIECE, PIECE), PIECE)
+        whole = slot_value[:, :, :, cols].reshape(64, PIECE)
+        extra = slot_value[:, :, :, WIDTH:].reshape(64, PIECE)
+        value = picked(late_backs, whole, extra, f)
+        usum[:, cols] = value[:TOK] + value[TOK:]
         return 0
 
-    def seconds(f, _):
-        bown[:, pl.ds(pl.multiple_of(f * PIECE, PIECE), PIECE)] = picked(2, f)
+    def late_slope(f, _):
+        cols = pl.ds(pl.multiple_of(f * PIECE, PIECE), PIECE)
+        whole = slot_tangent[:, :, :, cols].reshape(64, PIECE)
+        extra = slot_tangent[:, :, :, WIDTH // 2 :].reshape(64, PIECE)
+        aown[x_half, :, cols] += picked(late_backs, whole, extra, x_half * 4 + f)
         return 0
-
-    value_copy = pltpu.make_async_remote_copy(
-        src_ref=pown, dst_ref=prec, send_sem=e_send.at[0], recv_sem=e_recv.at[0], device_id=across
-    )
-    tangent_copy = pltpu.make_async_remote_copy(
-        src_ref=asend.at[1 - x_half], dst_ref=arec, send_sem=e_send.at[1], recv_sem=e_recv.at[1], device_id=across
-    )
-    lax.fori_loop(0, FOLD, values, 0)
-    value_copy.start()
-    lax.fori_loop(0, FOLD, tangents, 0)
-    tangent_copy.start()
-    lax.fori_loop(0, FOLD, seconds, 0)
 
     me = x_half * 2 + part
     lane = iota((16, 128), 1)
-    near = pl.ds(pl.multiple_of(x_half * (WIDTH // 2), WIDTH // 2), WIDTH // 2)
 
     def over(v):
         return jnp.sum(v, axis=-1, keepdims=True)
@@ -385,7 +463,7 @@
 
     def inner_value(block, _):
         at_ = pl.ds(pl.multiple_of(block * 16, 16), 16)
-        u = tokens_ref[at_].astype(f32) + (pown[at_].astype(f32) + prec[at_].astype(f32))
+        u = tokens_ref[at_].astype(f32) + (pown[at_].astype(f32) + prec[at_].astype(f32)) + usum[at_]
         usum[at_] = u
         gain = gain_ref[...]
         heavy = gain * gain * u
@@ -424,9 +502,13 @@
         stat[me, at_] = lay(stats, stat[me, at_])
         return 0
 
-    value_copy.wait_recv()
+    early_value().wait_recv()
+    late_value().wait_recv()
+    lax.fori_loop(0, FOLD, late_piece, 0)
     lax.fori_loop(0, TOK // 16, inner_value, 0)
-    tangent_copy.wait_recv()
+    early_tangent().wait_recv()
+    late_tangent().wait_recv()
+    lax.fori_loop(0, FOLD // 2, late_slope, 0)
     lax.fori_loop(0, TOK // 16, inner_tangent, 0)
 
     def stat_copy(i, who):
@@ -485,9 +567,6 @@
     for j in range(PLANES):
         end_dispatch(j)
         passed_on(j).wait_send()
-        for unit in (OWN, OTHER):
-            for i in range(3):
-                exchange(j, unit, i).wait_send()
         to_sibling(j).wait_send()
 
         def gone(q, _):
@@ -500,8 +579,11 @@
             return 0
 
         lax.fori_loop(0, 4, gone, 0)
-    value_copy.wait_send()
-    tangent_copy.wait_send()
+    for j, unit in UNITS:
+        for i in range(3):
+            exchange(j, unit, i).wait_send()
+    for copy in (early_value(), early_tangent(), late_value(), late_tangent()):
+        copy.wait_send()
     for i, who in enumerate((beside, across, diagonal)):
         stat_copy(i, who).wait_send()
     core_copy.wait_send()
@@ -511,9 +593,9 @@
         return 0
 
     lax.fori_loop(1, 16, end_all, 0)
-    final = jnp.sum(est_all[...], axis=0)
+    mean = jnp.sum(est_all[...], axis=0)
     small_ref[0:2, 0:TOK] = jnp.concatenate(curves, axis=0)
-    small_ref[2:3, :] = final[0:1] / jnp.maximum(final[1:2], 1.0)
+    small_ref[2:3, :] = mean[0:1] / jnp.maximum(mean[1:2], 1.0)
 
 
 def deliver(normed_in, small_in, normed_ref, curv_ref, est_ref):
@@ -554,16 +636,19 @@
             pltpu.VMEM((2 * TOK, WIDTH // 2), bf16),
             pltpu.VMEM((2 * TOK, WIDTH), f32),
             pltpu.VMEM((TOK, WIDTH), f32),
+            pltpu.VMEM((2, 2, MAIN, BLOCK), bf16),
+            pltpu.VMEM((2, 2, MAIN, WIDTH // 2 + PIECE), bf16),
+            pltpu.VMEM((2, MAIN, WIDTH // 2 + PIECE), bf16),
             pltpu.VMEM((4, TOK, 128), f32),
             pltpu.VMEM((2, 8, 128), f32),
             pltpu.VMEM((16, 8, 128), f32),
             dma((7,)),
             dma((PLANES, 4)), dma((PLANES, 4)),
             dma((PLANES,)), dma((PLANES,)),
-            dma((PLANES, 2, 3)), dma((PLANES, 2, 3)),
+            dma((PLANES, 3, 3)), dma((PLANES, 3, 3)),
             dma((PLANES,)), dma((PLANES,)),
             dma((PLANES, 4)), dma((PLANES, 4)),
-            dma((2,)), dma((2,)),
+            dma((4,)), dma((4,)),
             dma((3,)), dma((3,)),
             dma, dma,
             dma((16,)), dma((16,)),

time: 136 us -> 132 us (0.971)
  Pallas kernels: 136 us -> 131 us
    pallas_call x1, Pallas kernels: 134 us -> 130 us  [on_device(): pl.pallas_call(kernel, out_shape=(jax.ShapeDtypeStruct((TOK, WIDTH), bf16...]
where the time goes in v5:
time: 132 us
  Pallas kernels  131 us (99%)
    pallas_call x1, Pallas kernels, on_device(): pl.pallas_call(kernel, out_shape=(jax.ShapeDtypeStruct((TOK, WIDTH), bf16...  130 us

profile of v5, /device:TPU:1, one launch (start us, length us, event | category | flops | bytes accessed | tf_op | source)
XLA Modules:
  0.0 131.9 jit_solution(12408493955872233531)
XLA Ops:
  0.6 129.6 %shard_map.112 = (bf16[64,2048]{1,0:T(8,128)(2,1)}, f32[8,128]{1,0:T(8,128)}) custom-call(s32[2,64]{1,0:T(2,128)} %bitcast.6, f32[2,64]{1,0:T(2,128)} %bitcast.7, f32[1,2048]{1,0:T(1,128)} %bitcast.5, bf16[64,2048]{1,0:T(8,128)(2,1)} %tokens_ref.1, bf16[64,2048]{1,0:T(8,128)(2,1)} %targets_ref.1, bf16[2048,1024]{1,0:T(8,128)(2,1)} %wg_hbm.1, ...), custom_call_target="tpu_custom_call" | custom-call | tf_op jit(solution)/shard_map/pallas_call | solution.py:611
  130.3 1.7 %shard_map.113 = (bf16[64,2048]{1,0:T(8,128)(2,1)}, f32[2,64]{1,0:T(2,128)}, f32[1,8]{1,0:T(1,128)}) custom-call(bf16[64,2048]{1,0:T(8,128)(2,1)} %get-tuple-element.8.normed_in, f32[8,128]{1,0:T(8,128)} %get-tuple-element.9.small_in), custom_call_target="tpu_custom_call" | custom-call | tf_op jit(solution)/shard_map/pallas_call | solution.py:670

commit v6 on v5

--- a/solution.py
+++ b/solution.py
@@ -23,9 +23,11 @@
 HALF = HIDDEN // 2
 OWN = (0, 64)
 OTHER = (64, 80)
-OWN_A = (0, 32)
-OWN_B = (32, 32)
-UNITS = [(0, OWN), (0, OTHER), (1, OTHER), (1, OWN), (2, OTHER), (2, OWN), (3, OTHER), (3, OWN_A), (3, OWN_B)]
+PART_A = (0, 32)
+PART_B = (32, 32)
+UNITS = [(0, PART_A), (0, PART_B), (0, OTHER), (1, OTHER), (1, OWN), (2, OTHER), (2, OWN), (3, OTHER), (3, PART_A), (3, PART_B)]
+AHEAD = 4
+
 
 epsilon = 1e-05
 loss_weight = 8.0
@@ -124,7 +126,7 @@
     pl.semaphore_wait(barrier, 19)
 
     def plane_of(j, q):
-        return (z + (j + y + 2 * (q // 2)) % PLANES) % PLANES
+        return (z + (j + 2 * (y // 2) + 2 * (q // 2)) % PLANES) % PLANES
 
     def dispatch(j, q):
         target = plane_of(j, q) * 4 + q
@@ -170,12 +172,21 @@
             device_id=sibling,
         )
 
+    def owners(j, unit):
+        close = 2 * (y // 2)
+        away = 2 - close
+        if unit not in (PART_A, PART_B):
+            return (0, 1, 2, 3)
+        if j == 0:
+            return (close, close + 1) if unit == PART_A else (away, away + 1)
+        return (0, 2) if unit == PART_A else (1, 3)
+
+    def arrived(j, some):
+        for q in some:
+            pltpu.make_async_copy(out_rows.at[0], rows.at[j, core, q], d_recv.at[j, q]).wait()
+
     def arrive(j):
-        def one(q, _):
-            pltpu.make_async_copy(out_rows.at[0], rows.at[j, core, q], d_recv.at[j, q]).wait()
-            return 0
-
-        lax.fori_loop(0, 4, one, 0)
+        arrived(j, range(4))
         passed_on(j).start()
 
     a_, b_ = iota((128, 128), 0), iota((128, 128), 1)
@@ -185,7 +196,7 @@
 
     def exchange(j, unit, i):
         at_ = pl.ds(*unit)
-        number = {OWN: 0, OTHER: 1, OWN_A: 0, OWN_B: 2}[unit]
+        number = {OWN: 0, OTHER: 1, PART_A: 0, PART_B: 2}[unit]
         return pltpu.make_async_remote_copy(
             src_ref=tsend.at[j, i, at_], dst_ref=trecv.at[j, i, at_],
             send_sem=t_send.at[j, number, i], recv_sem=t_recv.at[j, number, i], device_id=beside,
@@ -195,7 +206,8 @@
         first, many = unit
         at_ = slice(first, first + many)
         if unit != OTHER:
-            lhs[at_, :] = rows[j, core, first // 16 : (first + many) // 16, :, :WIDTH].reshape(many, WIDTH)
+            for i, q in enumerate(owners(j, unit)):
+                lhs[first + 16 * i : first + 16 * i + 16, :] = rows[j, core, q, :, :WIDTH]
         else:
             passed_on(j).wait_recv()
             lhs[64:128, :] = rows[j, 1 - core, :, :, :WIDTH].reshape(64, WIDTH)
@@ -207,7 +219,7 @@
         def one(i, _):
             for half in range(2):
                 w = i * 2 + half
-                if j == 0 and unit == OWN:
+                if j == 0 and unit == PART_A:
                     pltpu.make_async_copy(w_in.at[w], w_in.at[w], w_sem.at[w]).wait()
                 tsend[j, i, at_, half * HALF : (half + 1) * HALF] = dot(lhs[at_, :], w_in[w]).astype(bf16)
             if send:
@@ -248,18 +260,17 @@
             return 0
 
         lax.fori_loop(0, many // 16, one, 0)
-        if j == 0 and unit == OWN:
+        if j == 0 and unit == PART_A:
             down.wait()
         whose = 1 - core if unit == OTHER else core
-        places = slice(0, 4) if unit == OTHER else slice(first // 16, (first + many) // 16)
-        whole = 64 if unit == OTHER else many
 
         def piece(n, _):
             cols = pl.ds(pl.multiple_of(n * PIECE, PIECE), PIECE)
             out = dot(jets[: 3 * many], w_down[:, cols]).astype(bf16)
             for i in range(3):
                 top = i * many
-                img[j, whose, places, i, :, cols] = out[top : top + whole].reshape(whole // 16, MAIN, PIECE)
+                for n_, q in enumerate(owners(j, unit)):
+                    img[j, whose, q, i, :, cols] = out[top + 16 * n_ : top + 16 * n_ + 16]
                 if unit == OTHER:
                     folded[i, pl.ds(pl.multiple_of(n * 16, 16), 16)] = out[top + 64 : top + 80]
             return 0
@@ -272,7 +283,7 @@
             to_sibling(j).start()
 
     def give(j, q):
-        target = ((z + PLANES - (j + q + 2 * (y // 2)) % PLANES) % PLANES) * 4 + q
+        target = ((z + PLANES - (j + 2 * (q // 2) + 2 * (y // 2)) % PLANES) % PLANES) * 4 + q
         here = pltpu.make_async_copy(img.at[j, core, q], ret.at[j, y], r_recv.at[j, y])
         there = pltpu.make_async_remote_copy(
             src_ref=img.at[j, core, q], dst_ref=ret.at[j, y], send_sem=r_send.at[j, q], recv_sem=r_recv.at[j, y],
@@ -280,11 +291,11 @@
         )
         return target == chip, here, there
 
-    def give_back(j, low=0, high=4):
-        if low == 0:
+    def give_back(j, some=(0, 1, 2, 3), first=True):
+        if first:
             to_sibling(j).wait_recv()
 
-        def one(q, _):
+        def one(q):
             img[j, core, q] = (img[j, core, q].astype(f32) + sib[j, q].astype(f32)).astype(bf16)
             mine, here, there = give(j, q)
 
@@ -296,9 +307,8 @@
             def _():
                 there.start()
 
-            return 0
-
-        lax.fori_loop(low, high, one, 0)
+        for q in some:
+            one(q)
 
     eye_tok = iota((TOK, TOK), 0) == iota((TOK, TOK), 1)
 
@@ -313,7 +323,7 @@
 
         def expert(line):
             j, pair = place(line)
-            return ((z + ((j + y + 2 * pair) & 3)) & 3) * 2 + pair
+            return ((z + ((j + 2 * (y // 2) + 2 * pair) & 3)) & 3) * 2 + pair
 
         spread = ones_where(expert(iota((many, EXPERTS), 0)) == iota((many, EXPERTS), 1)).astype(bf16)
         slot = dot(spread, count).astype(jnp.int32)
@@ -379,28 +389,30 @@
         early_tangent().start()
 
     start_dispatch(0)
-    arrive(0)
+    arrived(0, owners(0, PART_A))
     project(*UNITS[0], True)
-    for j in range(1, PLANES):
-        start_dispatch(j)
+    arrived(0, owners(0, PART_B))
+    passed_on(0).start()
+    start_dispatch(1)
     project(*UNITS[1], True)
+    project(*UNITS[2], True)
     arrive(1)
-    project(*UNITS[2], False)
-    arrive(2)
-    arrive(3)
+    start_dispatch(2)
+    start_dispatch(3)
+    project(*UNITS[3], True)
     for n, (j, unit) in enumerate(UNITS):
         last = n == len(UNITS) - 1
-        expand(j, unit, UNITS[n + 2] if n + 2 < len(UNITS) else None, send_early if last else None)
-        if n + 3 < len(UNITS):
-            project(*UNITS[n + 3], False)
-        if n == 2:
+        expand(j, unit, UNITS[n + 2] if AHEAD <= n + 2 < len(UNITS) else None, send_early if last else None)
+        if n < 2:
+            arrive(n + 2)
+        if n + 4 < len(UNITS):
+            project(*UNITS[n + 4], False)
+        if n == 3:
             give_back(0)
-        if j > 0 and unit == OWN:
+        if unit == OWN:
             give_back(j)
-        if unit == OWN_A:
-            give_back(j, 0, 2)
-        if unit == OWN_B:
-            give_back(j, 2, 4)
+        if j == 3 and unit != OTHER:
+            give_back(j, owners(j, unit), unit == PART_A)
         if (j, unit) == (3, OTHER):
             early()
 

time: 132 us -> 128 us (0.970)
  Pallas kernels: 131 us -> 127 us
    pallas_call x1, Pallas kernels: 130 us -> 125 us  [on_device(): pl.pallas_call(kernel, out_shape=(jax.ShapeDtypeStruct((TOK, WIDTH), bf16...]
where the time goes in v6:
time: 128 us
  Pallas kernels  127 us (99%)
    pallas_call x1, Pallas kernels, on_device(): pl.pallas_call(kernel, out_shape=(jax.ShapeDtypeStruct((TOK, WIDTH), bf16...  125 us

profile of v6, /device:TPU:1, one launch (start us, length us, event | category | flops | bytes accessed | tf_op | source)
XLA Modules:
  0.0 127.7 jit_solution(9125990125681834789)
XLA Ops:
  0.6 125.4 %shard_map.112 = (bf16[64,2048]{1,0:T(8,128)(2,1)}, f32[8,128]{1,0:T(8,128)}) custom-call(s32[2,64]{1,0:T(2,128)} %bitcast.6, f32[2,64]{1,0:T(2,128)} %bitcast.7, f32[1,2048]{1,0:T(1,128)} %bitcast.5, bf16[64,2048]{1,0:T(8,128)(2,1)} %tokens_ref.1, bf16[64,2048]{1,0:T(8,128)(2,1)} %targets_ref.1, bf16[2048,1024]{1,0:T(8,128)(2,1)} %wg_hbm.1, ...), custom_call_target="tpu_custom_call" | custom-call | tf_op jit(solution)/shard_map/pallas_call | solution.py:623
  126.0 1.7 %shard_map.113 = (bf16[64,2048]{1,0:T(8,128)(2,1)}, f32[2,64]{1,0:T(2,128)}, f32[1,8]{1,0:T(1,128)}) custom-call(bf16[64,2048]{1,0:T(8,128)(2,1)} %get-tuple-element.8.normed_in, f32[8,128]{1,0:T(8,128)} %get-tuple-element.9.small_in), custom_call_target="tpu_custom_call" | custom-call | tf_op jit(solution)/shard_map/pallas_call | solution.py:682

commit v7 on v6

--- a/solution.py
+++ b/solution.py
@@ -282,12 +282,16 @@
                 img[j, :, :, i, :, WIDTH:] = extra.reshape(2, 4, MAIN, PIECE)
             to_sibling(j).start()
 
-    def give(j, q):
+    def cuts(j):
+        return ((j, 0, 3),) if j < PLANES - 1 else ((j, 0, 2), (j + 1, 2, 1))
+
+    def give(j, q, cut):
+        number, low, many = cut
         target = ((z + PLANES - (j + 2 * (q // 2) + 2 * (y // 2)) % PLANES) % PLANES) * 4 + q
-        here = pltpu.make_async_copy(img.at[j, core, q], ret.at[j, y], r_recv.at[j, y])
+        src, dst = img.at[j, core, q, pl.ds(low, many)], ret.at[j, y, pl.ds(low, many)]
+        here = pltpu.make_async_copy(src, dst, r_recv.at[number, y])
         there = pltpu.make_async_remote_copy(
-            src_ref=img.at[j, core, q], dst_ref=ret.at[j, y], send_sem=r_send.at[j, q], recv_sem=r_recv.at[j, y],
-            device_id=at(target),
+            src_ref=src, dst_ref=dst, send_sem=r_send.at[number, q], recv_sem=r_recv.at[number, y], device_id=at(target)
         )
         return target == chip, here, there
 
@@ -295,9 +299,11 @@
         if first:
             to_sibling(j).wait_recv()
 
-        def one(q):
-            img[j, core, q] = (img[j, core, q].astype(f32) + sib[j, q].astype(f32)).astype(bf16)
-            mine, here, there = give(j, q)
+        def one(q, cut):
+            _, low, many = cut
+            own = slice(low, low + many)
+            img[j, core, q, own] = (img[j, core, q, own].astype(f32) + sib[j, q, own].astype(f32)).astype(bf16)
+            mine, here, there = give(j, q, cut)
 
             @pl.when(mine)
             def _():
@@ -307,8 +313,9 @@
             def _():
                 there.start()
 
-        for q in some:
-            one(q)
+        for cut in cuts(j):
+            for q in some:
+                one(q, cut)
 
     eye_tok = iota((TOK, TOK), 0) == iota((TOK, TOK), 1)
 
@@ -356,14 +363,16 @@
     def late_tangent():
         return across_copy(3, tangent_out, slot_tangent.at[x_half])
 
-    def returned(j):
+    def returned(j, cut):
+        number, low, many = cut
         for q in range(4):
-            pltpu.make_async_copy(ret.at[j, q], ret.at[j, q], r_recv.at[j, q]).wait()
+            block = ret.at[j, q, pl.ds(low, many)]
+            pltpu.make_async_copy(block, block, r_recv.at[number, q]).wait()
 
     def early():
         backs = back(64 * (PLANES - 1), lambda line: (line >> 6, (line >> 5) & 1))
         for j in range(PLANES - 1):
-            returned(j)
+            returned(j, cuts(j)[0])
 
         def piece(f, _):
             cols = pl.ds(pl.multiple_of(f * PIECE, PIECE), PIECE)
@@ -421,7 +430,7 @@
     far = pl.ds(pl.multiple_of((1 - x_half) * (WIDTH // 2), WIDTH // 2), WIDTH // 2)
     late_backs = back(64, lambda line: (final, (line >> 4) & 1))
     second_backs = back(64, lambda line: (final, (line >> 5) & 1))
-    returned(final)
+    returned(final, cuts(final)[0])
 
     def pair_sum(pair, i, cols):
         both = ret[final, 2 * pair, i, :, cols].astype(f32) + ret[final, 2 * pair + 1, i, :, cols].astype(f32)
@@ -437,6 +446,8 @@
     for pair in range(2):
         slot_tangent[x_half, pair, :, : WIDTH // 2] = pair_sum(pair, 1, near)
         slot_tangent[x_half, pair, :, WIDTH // 2 :] = pair_sum(pair, 1, slice(WIDTH, BLOCK))
+
+    returned(final, cuts(final)[1])
 
     def late_second(f, _):
         cols = pl.ds(pl.multiple_of(f * PIECE, PIECE), PIECE)
@@ -582,11 +593,12 @@
         to_sibling(j).wait_send()
 
         def gone(q, _):
-            mine, _, there = give(j, q)
-
-            @pl.when(jnp.logical_not(mine))
-            def _():
-                there.wait_send()
+            for cut in cuts(j):
+                mine, _, there = give(j, q, cut)
+
+                @pl.when(jnp.logical_not(mine))
+                def _():
+                    there.wait_send()
 
             return 0
 
@@ -659,7 +671,7 @@
             dma((PLANES,)), dma((PLANES,)),
             dma((PLANES, 3, 3)), dma((PLANES, 3, 3)),
             dma((PLANES,)), dma((PLANES,)),
-            dma((PLANES, 4)), dma((PLANES, 4)),
+            dma((PLANES + 1, 4)), dma((PLANES + 1, 4)),
             dma((4,)), dma((4,)),
             dma((3,)), dma((3,)),
             dma, dma,

time: 128 us -> 126 us (0.984)
    pallas_call x1, Pallas kernels: 125 us -> 124 us  [on_device(): pl.pallas_call(kernel, out_shape=(jax.ShapeDtypeStruct((TOK, WIDTH), bf16...]
where the time goes in v7:
time: 126 us
  Pallas kernels  126 us (100%)
    pallas_call x1, Pallas kernels, on_device(): pl.pallas_call(kernel, out_shape=(jax.ShapeDtypeStruct((TOK, WIDTH), bf16...  124 us

profile of v7, /device:TPU:1, one launch (start us, length us, event | category | flops | bytes accessed | tf_op | source)
XLA Modules:
  0.0 126.2 jit_solution(2306239923346869408)
XLA Ops:
  0.6 123.9 %shard_map.112 = (bf16[64,2048]{1,0:T(8,128)(2,1)}, f32[8,128]{1,0:T(8,128)}) custom-call(s32[2,64]{1,0:T(2,128)} %bitcast.6, f32[2,64]{1,0:T(2,128)} %bitcast.7, f32[1,2048]{1,0:T(1,128)} %bitcast.5, bf16[64,2048]{1,0:T(8,128)(2,1)} %tokens_ref.1, bf16[64,2048]{1,0:T(8,128)(2,1)} %targets_ref.1, bf16[2048,1024]{1,0:T(8,128)(2,1)} %wg_hbm.1, ...), custom_call_target="tpu_custom_call" | custom-call | tf_op jit(solution)/shard_map/pallas_call | solution.py:635
  124.5 1.7 %shard_map.113 = (bf16[64,2048]{1,0:T(8,128)(2,1)}, f32[2,64]{1,0:T(2,128)}, f32[1,8]{1,0:T(1,128)}) custom-call(bf16[64,2048]{1,0:T(8,128)(2,1)} %get-tuple-element.8.normed_in, f32[8,128]{1,0:T(8,128)} %get-tuple-element.9.small_in), custom_call_target="tpu_custom_call" | custom-call | tf_op jit(solution)/shard_map/pallas_call | solution.py:694
